TPU v7x, 128 devices: a whole 4x4x4 slice. The times are simulated.
128 devices in a mesh: ctx: 16 (over y, x_lo, core), fsdp: 8 (over x_hi, z).
Axes of the slice: x: 4 (x_hi: 2, x_lo: 2; x = x_hi * 2 + x_lo), y: 4, z: 4, core: 2. Of those that a mesh axis runs over, the one named last changes fastest.
Arguments:
- tokens: bfloat16 [8, 2048, 1536], P('fsdp', 'ctx'), may hold values from -6 to 6
- cotangent: bfloat16 [8, 2048, 1536], P('fsdp', 'ctx'), may hold values from -6 to 6
- routes: int32 [8, 2048, 6], P('fsdp', 'ctx'), may hold values from 0 to 63, all different within a row; in each aligned block of 128 rows (0 to 127, 128 to 255, ..., all dimensions but the last counted through in order) at most 24 rows name the same one
- gates: float32 [8, 2048, 6], P('fsdp', 'ctx'), may hold values from 0.08 to 0.25
- attn_gain: bfloat16 [1536], P(('ctx', 'fsdp')), may hold values from 0.5 to 1.5
- ffn_gain: bfloat16 [1536], P(('ctx', 'fsdp')), may hold values from 0.5 to 1.5
- w_query: bfloat16 [1536, 1536], P(('ctx', 'fsdp')), may hold values from -0.15625 to 0.15625
- key_weight_matrix: bfloat16 [1536, 512], P(('ctx', 'fsdp')), may hold values from -0.15625 to 0.15625
- value_weight_matrix: bfloat16 [1536, 512], P(('ctx', 'fsdp')), may hold values from -0.15625 to 0.15625
- w_out: bfloat16 [1536, 1536], P(None, ('ctx', 'fsdp')), may hold values from -3.5 to 3.5
- shared_gate: bfloat16 [1536, 1024], P(('ctx', 'fsdp')), may hold values from -0.15625 to 0.15625
- shared_up: bfloat16 [1536, 1024], P(('ctx', 'fsdp')), may hold values from -0.15625 to 0.15625
- shared_down: bfloat16 [1024, 1536], P(None, ('ctx', 'fsdp')), may hold values from -0.375 to 0.375
- expert_gate: bfloat16 [64, 1536, 512], P('ctx', 'fsdp'), may hold values from -0.15625 to 0.15625
- expert_up: bfloat16 [64, 1536, 512], P('ctx', 'fsdp'), may hold values from -0.15625 to 0.15625
- expert_down: bfloat16 [64, 512, 1536], P('ctx', None, 'fsdp'), may hold values from -1 to 1
Outputs:
- layer_out: bfloat16 [8, 2048, 1536], P('fsdp', 'ctx')
- input_grad: float32 [8, 2048, 1536], P('fsdp', 'ctx')
- attn_gain_grad: float32 [1536], P(('ctx', 'fsdp'))
- ffn_gain_grad: float32 [1536], P(('ctx', 'fsdp'))
- w_query_grad: float32 [1536, 1536], P(('ctx', 'fsdp'))
- w_key_grad: float32 [1536, 512], P(('ctx', 'fsdp'))
- w_value_grad: float32 [1536, 512], P(('ctx', 'fsdp'))
- w_out_grad: float32 [1536, 1536], P(None, ('ctx', 'fsdp'))
- shared_gate_grad: float32 [1536, 1024], P(('ctx', 'fsdp'))
- shared_up_grad: float32 [1536, 1024], P(('ctx', 'fsdp'))
- shared_down_grad: float32 [1024, 1536], P(None, ('ctx', 'fsdp'))
- expert_gate_grad: float32 [64, 1536, 512], P('ctx', 'fsdp')
- expert_up_grad: float32 [64, 1536, 512], P('ctx', 'fsdp')
- expert_down_grad: float32 [64, 512, 1536], P('ctx', None, 'fsdp')
Inputs may be any that keep to these rules, and one draw needn't show every extreme that they name: `routes`: each row names 6 different experts. Among the rows of one device (an aligned block of 128 positions of a sequence) no expert is named more than 24 times, and in every draw some device's rows name one expert exactly 24 times.
All inputs are finite; a program needn't handle non-finite values.
Results may differ from a plain program's by a relative error of at most 0.04.
Values may be sent and summed in bfloat16 or wider, within the bound.
A program may use at most 256 MiB of HBM per device.

v0:
```python
import jax
import jax.numpy as jnp
from jax import lax
from jax.sharding import PartitionSpec as P

HEAD_DIMENSION = 128


EPS = 1e-05


def matmul(left_mat, right_mat):
    return jnp.dot(left_mat, right_mat, preferred_element_type=jnp.float32)


def matmul_trans(left_mat, right_mat):
    return lax.dot_general(
        left_mat, right_mat, (((1,), (1,)), ((), ())), preferred_element_type=jnp.float32
    )


def weight_grad(left_mat, right_mat):
    return lax.dot_general(
        left_mat, right_mat, (((0,), (0,)), ((), ())), preferred_element_type=jnp.float32
    )


def silu_parts(pre_act):
    sigmoid_v = jax.nn.sigmoid(pre_act)
    return (pre_act * sigmoid_v, sigmoid_v * (1.0 + pre_act * (1.0 - sigmoid_v)))


def norm_forward(values, gain_vec):
    inverse = lax.rsqrt(jnp.mean(values * values, -1, keepdims=True) + EPS)
    scaled = values * inverse
    return (scaled * gain_vec, scaled, inverse)


def norm_backward(grad_in, scaled, inverse, gain_vec):
    gain_grad = jnp.sum(grad_in * scaled, 0)
    inner_grad = grad_in * gain_vec
    return (
        inverse * (inner_grad - scaled * jnp.mean(inner_grad * scaled, -1, keepdims=True)),
        gain_grad,
    )


def local(
    tokens,
    cotangent,
    routes,
    gates,
    attn_gain,
    ffn_gain,
    w_query,
    key_weight_matrix,
    value_weight_matrix,
    w_out,
    shared_gate,
    shared_up,
    shared_down,
    expert_gate,
    expert_up,
    expert_down,
):
    ctx_size = lax.axis_size("ctx")
    ctx_rank = lax.axis_index("ctx")
    (
        gain_one,
        gain_two,
        query_full,
        key_full,
        value_full,
        out_full,
        sgate_full,
        sup_full,
        sdown_full,
    ) = (
        lax.all_gather(attn_gain, ("ctx", "fsdp"), axis=0, tiled=True),
        lax.all_gather(ffn_gain, ("ctx", "fsdp"), axis=0, tiled=True),
        lax.all_gather(w_query, ("ctx", "fsdp"), axis=0, tiled=True),
        lax.all_gather(key_weight_matrix, ("ctx", "fsdp"), axis=0, tiled=True),
        lax.all_gather(value_weight_matrix, ("ctx", "fsdp"), axis=0, tiled=True),
        lax.all_gather(w_out, ("ctx", "fsdp"), axis=1, tiled=True),
        lax.all_gather(shared_gate, ("ctx", "fsdp"), axis=0, tiled=True),
        lax.all_gather(shared_up, ("ctx", "fsdp"), axis=0, tiled=True),
        lax.all_gather(shared_down, ("ctx", "fsdp"), axis=1, tiled=True),
    )
    expert_gate_gathered, expert_up_gathered, expert_down_gathered = (
        lax.all_gather(expert_gate, "fsdp", axis=1, tiled=True),
        lax.all_gather(expert_up, "fsdp", axis=1, tiled=True),
        lax.all_gather(expert_down, "fsdp", axis=2, tiled=True),
    )
    gain_one_f = gain_one.astype(jnp.float32)
    gain_two_f = gain_two.astype(jnp.float32)
    tok_rows = tokens.shape[1]
    model_width = tokens.shape[2]
    route_count = routes.shape[2]
    inputs = tokens.reshape(tok_rows, model_width).astype(jnp.float32)
    grad_out = cotangent.reshape(tok_rows, model_width)
    grad_f = grad_out.astype(jnp.float32)
    route_weights = gates.reshape(tok_rows, route_count)
    normed_one, scaled_one, inverse_one = norm_forward(inputs, gain_one_f)
    hidden_one = normed_one.astype(jnp.bfloat16)
    queries = matmul(hidden_one, query_full).astype(jnp.bfloat16)
    keys = matmul(hidden_one, key_full).astype(jnp.bfloat16)
    values = matmul(hidden_one, value_full).astype(jnp.bfloat16)
    kv_heads = keys.shape[1] // HEAD_DIMENSION
    groups = queries.shape[1] // keys.shape[1]
    score_scale = HEAD_DIMENSION ** (-0.5)
    query_heads = queries.reshape(tok_rows, kv_heads, groups, HEAD_DIMENSION)
    query_pos = ctx_rank * tok_rows + jnp.arange(tok_rows, dtype=jnp.int32)
    run_max = jnp.full((kv_heads, groups, tok_rows), -1e30, jnp.float32)
    piece_keys = lax.all_gather(keys, "ctx", axis=0, tiled=True)
    piece_values = lax.all_gather(values, "ctx", axis=0, tiled=True)
    piece_rows = piece_keys.shape[0]
    key_heads = piece_keys.reshape(piece_rows, kv_heads, HEAD_DIMENSION)
    value_heads = piece_values.reshape(piece_rows, kv_heads, HEAD_DIMENSION)
    scores = (
        jnp.einsum("tkgd,rkd->kgtr", query_heads, key_heads, preferred_element_type=jnp.float32)
        * score_scale
    )
    allowed = jnp.arange(piece_rows, dtype=jnp.int32)[None, :] <= query_pos[:, None]
    scores = jnp.where(allowed, scores, -jnp.inf)
    new_max = jnp.maximum(run_max, jnp.max(scores, -1))
    softmax_w = jnp.exp(scores - new_max[..., None])
    new_sum = jnp.sum(softmax_w, -1)
    new_acc = jnp.einsum(
        "kgtr,rkd->kgtd",
        softmax_w.astype(jnp.bfloat16),
        value_heads,
        preferred_element_type=jnp.float32,
    )
    head_out = new_acc / new_sum[..., None]
    log_total = new_max + jnp.log(new_sum)
    attended = (
        jnp.transpose(head_out, (2, 0, 1, 3))
        .reshape(tok_rows, queries.shape[1])
        .astype(jnp.bfloat16)
    )
    resid_one = inputs + matmul(attended, out_full)
    normed_two, scaled_two, inverse_two = norm_forward(resid_one, gain_two_f)
    hidden_two = normed_two.astype(jnp.bfloat16)
    exp_dev = expert_gate.shape[0]
    experts_total = exp_dev * ctx_size
    capacity = 2 * tok_rows * route_count // experts_total
    flat_ids = routes.reshape(tok_rows * route_count)
    onehot = (flat_ids[:, None] == jnp.arange(experts_total, dtype=jnp.int32)[None, :]).astype(
        jnp.int32
    )
    slot_index = jnp.sum(onehot * jnp.cumsum(onehot, 0), 1) - 1
    target = flat_ids * capacity + slot_index
    route_rows = jnp.repeat(hidden_two, route_count, 0)
    outgoing = (
        jnp.zeros((experts_total * capacity, model_width), jnp.bfloat16).at[target].set(route_rows)
    )
    received_parts = lax.all_to_all(
        outgoing.reshape(ctx_size, exp_dev, capacity, model_width),
        "ctx",
        split_axis=0,
        concat_axis=0,
        tiled=True,
    )
    gate_pre = jnp.einsum(
        "qtmp,tpy->qtmy", received_parts, expert_gate_gathered, preferred_element_type=jnp.float32
    )
    up_preactivation = jnp.einsum(
        "qtmp,tpy->qtmy", received_parts, expert_up_gathered, preferred_element_type=jnp.float32
    )
    gate_act, gate_slope = silu_parts(gate_pre)
    expert_hidden = (gate_act * up_preactivation).astype(jnp.bfloat16)
    expert_rows = jnp.einsum(
        "sech,ehd->secd", expert_hidden, expert_down_gathered, preferred_element_type=jnp.float32
    ).astype(jnp.bfloat16)
    returned = lax.all_to_all(expert_rows, "ctx", split_axis=0, concat_axis=0, tiled=True).reshape(
        experts_total * capacity, model_width
    )
    route_out = returned[target].reshape(tok_rows, route_count, model_width).astype(jnp.float32)
    combined = jnp.sum(route_out * route_weights[:, :, None], 1)
    shared_gate_pre = matmul(hidden_two, sgate_full)
    shared_up_pre = matmul(hidden_two, sup_full)
    shared_act, shared_slope = silu_parts(shared_gate_pre)
    shared_hidden = (shared_act * shared_up_pre).astype(jnp.bfloat16)
    shared_out = matmul(shared_hidden, sdown_full)
    layer_out = (resid_one + combined + shared_out).astype(jnp.bfloat16)
    route_grads = (
        jnp.repeat(grad_f, route_count, 0) * route_weights.reshape(tok_rows * route_count, 1)
    ).astype(jnp.bfloat16)
    outgoing_grads = (
        jnp.zeros((experts_total * capacity, model_width), jnp.bfloat16).at[target].set(route_grads)
    )
    arrived_grads = lax.all_to_all(
        outgoing_grads.reshape(ctx_size, exp_dev, capacity, model_width),
        "ctx",
        split_axis=0,
        concat_axis=0,
        tiled=True,
    )
    hidden_grad = jnp.einsum(
        "secd,ehd->sech", arrived_grads, expert_down_gathered, preferred_element_type=jnp.float32
    )
    grad_edown = jnp.einsum(
        "sech,secd->ehd", expert_hidden, arrived_grads, preferred_element_type=jnp.float32
    )
    gate_grad = (hidden_grad * up_preactivation * gate_slope).astype(jnp.bfloat16)
    up_branch_gradient = (hidden_grad * gate_act).astype(jnp.bfloat16)
    grad_egate = jnp.einsum(
        "bpwg,bpwx->pgx", received_parts, gate_grad, preferred_element_type=jnp.float32
    )
    expert_up_weight_gradient = jnp.einsum(
        "bpwg,bpwx->pgx", received_parts, up_branch_gradient, preferred_element_type=jnp.float32
    )
    row_grads = jnp.einsum(
        "kfau,fvu->kfav", gate_grad, expert_gate_gathered, preferred_element_type=jnp.float32
    )
    row_grads = (
        row_grads
        + jnp.einsum(
            "kfau,fvu->kfav",
            up_branch_gradient,
            expert_up_gathered,
            preferred_element_type=jnp.float32,
        )
    ).astype(jnp.bfloat16)
    returned_grads = lax.all_to_all(
        row_grads, "ctx", split_axis=0, concat_axis=0, tiled=True
    ).reshape(experts_total * capacity, model_width)
    expert_gate_shard, expert_up_shard, expert_down_shard = (
        lax.psum_scatter(
            grad_egate.astype(jnp.bfloat16), "fsdp", scatter_dimension=1, tiled=True
        ).astype(jnp.float32),
        lax.psum_scatter(
            expert_up_weight_gradient.astype(jnp.bfloat16), "fsdp", scatter_dimension=1, tiled=True
        ).astype(jnp.float32),
        lax.psum_scatter(
            grad_edown.astype(jnp.bfloat16), "fsdp", scatter_dimension=2, tiled=True
        ).astype(jnp.float32),
    )
    shared_hidden_grad = matmul_trans(grad_out, sdown_full)
    grad_sdown = weight_grad(shared_hidden, grad_out)
    shared_gate_grad = (shared_hidden_grad * shared_up_pre * shared_slope).astype(jnp.bfloat16)
    shared_up_grad = (shared_hidden_grad * shared_act).astype(jnp.bfloat16)
    grad_sgate = weight_grad(hidden_two, shared_gate_grad)
    grad_sup = weight_grad(hidden_two, shared_up_grad)
    hidden_two_grad = matmul_trans(shared_gate_grad, sgate_full) + matmul_trans(
        shared_up_grad, sup_full
    )
    hidden_two_grad = hidden_two_grad + jnp.sum(
        returned_grads[target].reshape(tok_rows, route_count, model_width).astype(jnp.float32), 1
    )
    resid_part, grad_gain_two = norm_backward(hidden_two_grad, scaled_two, inverse_two, gain_two_f)
    resid_grad = grad_f + resid_part
    attn_grad = resid_grad.astype(jnp.bfloat16)
    grad_wout = weight_grad(attended, attn_grad)
    attended_grad = matmul_trans(attn_grad, out_full).astype(jnp.bfloat16)
    key_all, value_all = (
        lax.all_gather(keys, "ctx", axis=0, tiled=True),
        lax.all_gather(values, "ctx", axis=0, tiled=True),
    )
    grad_heads = attended_grad.reshape(tok_rows, kv_heads, groups, HEAD_DIMENSION)
    delta_sum = jnp.sum(jnp.transpose(grad_heads.astype(jnp.float32), (1, 2, 0, 3)) * head_out, -1)
    seq_len = key_all.shape[0]
    key_block = min(512, seq_len)
    key_blocks = key_all.reshape(seq_len // key_block, key_block, kv_heads, HEAD_DIMENSION)
    value_blocks = value_all.reshape(seq_len // key_block, key_block, kv_heads, HEAD_DIMENSION)
    block_starts = jnp.arange(seq_len // key_block, dtype=jnp.int32) * key_block

    def back_block(query_acc, block_item):
        keys_here, values_here, first_row = block_item
        scores = (
            jnp.einsum("tkgd,rkd->kgtr", query_heads, keys_here, preferred_element_type=jnp.float32)
            * score_scale
        )
        allowed = (first_row + jnp.arange(key_block, dtype=jnp.int32))[None, :] <= query_pos[
            :, None
        ]
        softmax_w = jnp.where(allowed, jnp.exp(scores - log_total[..., None]), 0.0)
        weight_grads = jnp.einsum(
            "tkgd,rkd->kgtr", grad_heads, values_here, preferred_element_type=jnp.float32
        )
        score_grad = (softmax_w * (weight_grads - delta_sum[..., None])).astype(jnp.bfloat16)
        value_term = jnp.einsum(
            "kgtr,tkgd->rkd",
            softmax_w.astype(jnp.bfloat16),
            grad_heads,
            preferred_element_type=jnp.float32,
        )
        key_term = (
            jnp.einsum(
                "kgtr,tkgd->rkd", score_grad, query_heads, preferred_element_type=jnp.float32
            )
            * score_scale
        )
        query_acc = query_acc + jnp.einsum(
            "kgtr,rkd->tkgd", score_grad, keys_here, preferred_element_type=jnp.float32
        )
        return (query_acc, (key_term, value_term))

    query_acc, (key_terms, value_terms) = lax.scan(
        back_block,
        jnp.zeros((tok_rows, kv_heads, groups, HEAD_DIMENSION), jnp.float32),
        (key_blocks, value_blocks, block_starts),
    )
    key_grad, value_grad = (
        lax.psum_scatter(
            key_terms.reshape(seq_len, kv_heads * HEAD_DIMENSION).astype(jnp.bfloat16),
            "ctx",
            scatter_dimension=0,
            tiled=True,
        ).astype(jnp.float32),
        lax.psum_scatter(
            value_terms.reshape(seq_len, kv_heads * HEAD_DIMENSION).astype(jnp.bfloat16),
            "ctx",
            scatter_dimension=0,
            tiled=True,
        ).astype(jnp.float32),
    )
    query_grad = (query_acc * score_scale).reshape(tok_rows, queries.shape[1]).astype(jnp.bfloat16)
    key_grad = key_grad.astype(jnp.bfloat16)
    value_grad = value_grad.astype(jnp.bfloat16)
    hidden_one_grad = (
        matmul_trans(query_grad, query_full)
        + matmul_trans(key_grad, key_full)
        + matmul_trans(value_grad, value_full)
    )
    grad_wquery = weight_grad(hidden_one, query_grad)
    grad_wkey = weight_grad(hidden_one, key_grad)
    grad_wvalue = weight_grad(hidden_one, value_grad)
    input_part, grad_gain_one = norm_backward(hidden_one_grad, scaled_one, inverse_one, gain_one_f)
    input_grad = resid_grad + input_part
    dense_parts = (
        lax.psum_scatter(grad_gain_one, ("ctx", "fsdp"), scatter_dimension=0, tiled=True),
        lax.psum_scatter(grad_gain_two, ("ctx", "fsdp"), scatter_dimension=0, tiled=True),
        lax.psum_scatter(grad_wquery, ("ctx", "fsdp"), scatter_dimension=0, tiled=True),
        lax.psum_scatter(grad_wkey, ("ctx", "fsdp"), scatter_dimension=0, tiled=True),
        lax.psum_scatter(grad_wvalue, ("ctx", "fsdp"), scatter_dimension=0, tiled=True),
        lax.psum_scatter(grad_wout, ("ctx", "fsdp"), scatter_dimension=1, tiled=True),
        lax.psum_scatter(grad_sgate, ("ctx", "fsdp"), scatter_dimension=0, tiled=True),
        lax.psum_scatter(grad_sup, ("ctx", "fsdp"), scatter_dimension=0, tiled=True),
        lax.psum_scatter(grad_sdown, ("ctx", "fsdp"), scatter_dimension=1, tiled=True),
    )
    return (
        layer_out.reshape(1, tok_rows, model_width),
        input_grad.reshape(1, tok_rows, model_width),
        dense_parts[0],
        dense_parts[1],
        dense_parts[2],
        dense_parts[3],
        dense_parts[4],
        dense_parts[5],
        dense_parts[6],
        dense_parts[7],
        dense_parts[8],
        expert_gate_shard,
        expert_up_shard,
        expert_down_shard,
    )


def solution(mesh):
    return jax.shard_map(
        local,
        mesh=mesh,
        in_specs=(
            P("fsdp", "ctx", None),
            P("fsdp", "ctx", None),
            P("fsdp", "ctx", None),
            P("fsdp", "ctx", None),
            P(("ctx", "fsdp")),
            P(("ctx", "fsdp")),
            P(("ctx", "fsdp"), None),
            P(("ctx", "fsdp"), None),
            P(("ctx", "fsdp"), None),
            P(None, ("ctx", "fsdp")),
            P(("ctx", "fsdp"), None),
            P(("ctx", "fsdp"), None),
            P(None, ("ctx", "fsdp")),
            P("ctx", "fsdp", None),
            P("ctx", "fsdp", None),
            P("ctx", None, "fsdp"),
        ),
        out_specs=(
            P("fsdp", "ctx", None),
            P("fsdp", "ctx", None),
            P(("ctx", "fsdp")),
            P(("ctx", "fsdp")),
            P(("ctx", "fsdp"), None),
            P(("ctx", "fsdp"), None),
            P(("ctx", "fsdp"), None),
            P(None, ("ctx", "fsdp")),
            P(("ctx", "fsdp"), None),
            P(("ctx", "fsdp"), None),
            P(None, ("ctx", "fsdp")),
            P("ctx", "fsdp", None),
            P("ctx", "fsdp", None),
            P("ctx", None, "fsdp"),
        ),
        check_vma=False,
    )
```

profile of v0, /device:TPU:0, one launch (start us, length us, event | category | flops | bytes accessed | tf_op | source)
XLA Modules:
  0.0 4805.8 jit_solution(15869269639995188034)
XLA Ops:
  10.4 68.4 %all-reduce.19 = (bf16[1536]{0:T(1024)(128)(2,1)S(1)}, bf16[1536]{0:T(1024)(128)(2,1)S(1)}) all-reduce(bf16[1536]{0:T(1024)(128)(2,1)S(1)} %dynamic-update-slice, bf16[1536]{0:T(1024)(128)(2,1)S(1)} %dynamic-update-slice.1), channel_id=1, replica_groups=mesh['ctx'=16,'fsdp'=8] {'ctx','fsdp'}, use_global_device_ids=true, to_apply=%add | all-reduce | flops 3072 | bytes 12288
  80.0 231.2 %all-gather.30.cloned.1.call-done = bf16[128,12,512]{2,1,0:T(8,128)(2,1)} async-done(((bf16[1,12,512]{2,1,0:T(8,128)(2,1)}), bf16[128,12,512]{2,1,0:T(8,128)(2,1)}) %all-gather.30.cloned.1.call-update) | async-done | bytes 1572880 | tf_op jit(solution)/shard_map/all_gather | solution.py:82
  315.0 299.3 %all-gather.34.cloned.1.call-done = bf16[128,12,512]{2,1,0:T(8,128)(2,1)} async-done(((bf16[1,12,512]{2,1,0:T(8,128)(2,1)}), bf16[128,12,512]{2,1,0:T(8,128)(2,1)}) %all-gather.34.cloned.1.call-update) | async-done | bytes 1572880 | tf_op jit(solution)/shard_map/all_gather | solution.py:83
  625.9 26.0 all-gather.20.cloned.1.call-done
  656.0 32.3 all-gather.22.cloned.1.call-done
  691.2 309.2 %all-gather.32.cloned.1.call-done = bf16[128,12,1536]{2,1,0:T(8,128)(2,1)} async-done(((bf16[1,12,1536]{2,1,0:T(8,128)(2,1)}), bf16[128,12,1536]{2,1,0:T(8,128)(2,1)}) %all-gather.32.cloned.1.call-update) | async-done | bytes 4718608 | tf_op jit(solution)/shard_map/all_gather | solution.py:81
  1011.9 301.1 %all-gather.36.cloned.1.call-done = bf16[128,12,1536]{2,1,0:T(8,128)(2,1)} async-done(((bf16[1,12,1536]{2,1,0:T(8,128)(2,1)}), bf16[128,12,1536]{2,1,0:T(8,128)(2,1)}) %all-gather.36.cloned.1.call-update) | async-done | bytes 4718608 | tf_op jit(solution)/shard_map/all_gather | solution.py:84
  1378.0 64.2 %all-to-all-done = bf16[16,4,24,1536]{3,2,1,0:T(8,128)(2,1)} async-done(((bf16[16,4,24,1536]{3,2,1,0:T(8,128)(2,1)}), bf16[16,4,24,1536]{3,2,1,0:T(8,128)(2,1)}, u32[]{:S(2)}, u32[]{:S(2)}) %all-to-all-start) | async-done | bytes 4718624 | tf_op jit(solution)/shard_map/all_to_all | solution.py:157
  1454.5 104.0 %all-gather.24.cloned.1.call-done = bf16[4,1536,512]{2,1,0:T(8,128)(2,1)} async-done(((bf16[4,192,512]{2,1,0:T(8,128)(2,1)}), bf16[4,1536,512]{2,1,0:T(8,128)(2,1)}) %all-gather.24.cloned.1.call-update) | async-done | bytes 6291472 | tf_op jit(solution)/shard_map/all_gather | solution.py:90
  1567.0 80.8 %all-gather.28.cloned.1.call-done = bf16[4,512,1536]{1,2,0:T(8,128)(2,1)} async-done(((bf16[4,512,192]{1,2,0:T(8,128)(2,1)}), bf16[4,512,1536]{1,2,0:T(8,128)(2,1)}) %all-gather.28.cloned.1.call-update) | async-done | bytes 6291472 | tf_op jit(solution)/shard_map/all_gather | solution.py:92
  1682.6 296.6 %all-gather.38.cloned.1.call-done = bf16[128,12,1024]{2,1,0:T(8,128)(2,1)} async-done(((bf16[1,12,1024]{2,1,0:T(8,128)(2,1)}), bf16[128,12,1024]{2,1,0:T(8,128)(2,1)}) %all-gather.38.cloned.1.call-update) | async-done | bytes 3145744 | tf_op jit(solution)/shard_map/all_gather | solution.py:85
  1985.5 306.1 %all-gather.40.cloned.1.call-done = bf16[128,12,1024]{2,1,0:T(8,128)(2,1)} async-done(((bf16[1,12,1024]{2,1,0:T(8,128)(2,1)}), bf16[128,12,1024]{2,1,0:T(8,128)(2,1)}) %all-gather.40.cloned.1.call-update) | async-done | bytes 3145744 | tf_op jit(solution)/shard_map/all_gather | solution.py:86
  2296.3 304.5 %all-gather.42.cloned.1.call-done = bf16[128,12,1024]{2,1,0:T(8,128)(2,1)} async-done(((bf16[1,12,1024]{2,1,0:T(8,128)(2,1)}), bf16[128,12,1024]{2,1,0:T(8,128)(2,1)}) %all-gather.42.cloned.1.call-update) | async-done | bytes 3145744 | tf_op jit(solution)/shard_map/all_gather | solution.py:87
  2652.3 40.0 while.15
  2732.8 471.7 %fusion.8 = f32[1024,16]{0,1:T(8,128)} fusion(f32[1024,1536]{0,1:T(8,128)} %fusion.103), kind=kCustom, calls=%all-reduce-scatter.6 | all-reduce-scatter fusion | flops 2097153 | bytes 6356992
  3266.1 24.5 collective-permute-done.218
  3384.0 554.9 %fusion.125 = (f32[16,1536]{1,0:T(8,128)}, f32[16,512]{1,0:T(8,128)}, f32[16,512]{1,0:T(8,128)}, f32[1536,16]{0,1:T(8,128)}, f32[16,1024]{1,0:T(8,128)}, /*index=5*/f32[16,1024]{1,0:T(8,128)}) fusion(f32[1536,1536]{1,0:T(8,128)} %fusion.101, f32[1536,512]{1,0:T(8,128)S(1)} %fusion.120, f32[1536,512]{1,0:T(8,128)} %fusion.118, f32[1536,1536]{0,1:T(8,128)} %fusion.111, ...), kind=kCustom, calls=%all-reduce-scatter.7 | all-reduce-scatter fusion | flops 12582913 | bytes 38141952
  4275.6 30.2 concatenate.6
  4444.0 65.4 %all-reduce.18 = (f32[1536]{0:T(1024)S(1)}, f32[1536]{0:T(1024)S(1)}) all-reduce(f32[1536]{0:T(1024)S(1)} %get-tuple-element.161, f32[1536]{0:T(1024)S(1)} %copy-done.217), channel_id=4, replica_groups=mesh['ctx'=16,'fsdp'=8] {'ctx','fsdp'}, use_global_device_ids=true, to_apply=%region_19.20.clone | all-reduce | flops 3072 | bytes 24576
  4526.7 25.9 concatenate.2
  4589.6 49.6 %concatenate.4 = f32[524,1024]{1,0:T(8,128)} concatenate(f32[12,1024]{1,0:T(8,128)S(1)} %copy-done.125, f32[16,1024]{1,0:T(8,128)S(1)} %copy-done.123, f32[16,1024]{1,0:T(8,128)S(1)} %copy-done.127, f32[16,1024]{1,0:T(8,128)} %copy-done.128, f32[16,1024]{1,0:T(8,128)} %copy-done.129, f32[16,1024]{1,0:T(8,128)} %copy-done.130, f32[16,1024]{1,0:T(8,128)} %copy-done.131, ...), dimensions={0} | concatenate | bytes 4292608
  4639.1 29.5 concatenate.5
  4705.7 30.9 concatenate
  4736.7 52.6 %concatenate.3 = f32[1536,524]{0,1:T(8,128)} concatenate(f32[1536,12]{0,1:T(8,128)S(1)} %copy-done.53, f32[1536,16]{0,1:T(8,128)} %copy-done.81, f32[1536,16]{0,1:T(8,128)} %copy-done.84, f32[1536,16]{0,1:T(8,128)} %copy-done.85, f32[1536,16]{0,1:T(8,128)} %copy-done.86, f32[1536,16]{0,1:T(8,128)} %copy-done.87, f32[1536,16]{0,1:T(8,128)} %copy-done.88, f32[1536,16]{0,1:T(8,128)} %copy-done.89, ...), dimensions={1} | concatenate | bytes 6438912
  (1172 shorter events, 1026.5 us)
Async XLA Ops:
  7.2 304.0 %all-gather.30.cloned.1.call-start = ((), (), s32[]{:S(2)}) async-start(), calls=%async_computation.19 | async-start | bytes 2113536 | tf_op jit(solution)/shard_map/all_gather | solution.py:82
  7.9 606.4 %all-gather.34.cloned.1.call-start = ((), (), s32[]{:S(2)}) async-start(), calls=%async_computation.21 | async-start | bytes 2113536 | tf_op jit(solution)/shard_map/all_gather | solution.py:83
  8.7 643.3 %all-gather.20.cloned.1.call-start = ((), (), s32[]{:S(2)}) async-start(), calls=%async_computation.9 | async-start | bytes 2228224 | tf_op jit(solution)/shard_map/all_gather | solution.py:114
  314.9 373.3 %all-gather.22.cloned.1.call-start = ((), (), s32[]{:S(2)}) async-start(), calls=%async_computation.10 | async-start | bytes 2228224 | tf_op jit(solution)/shard_map/all_gather | solution.py:115
  618.0 382.3 %all-gather.32.cloned.1.call-start = ((), (), s32[]{:S(2)}) async-start(), calls=%async_computation.20 | async-start | bytes 6340608 | tf_op jit(solution)/shard_map/all_gather | solution.py:81
  618.6 694.5 %all-gather.36.cloned.1.call-start = ((), (), s32[]{:S(2)}) async-start(), calls=%async_computation.22 | async-start | bytes 6340608 | tf_op jit(solution)/shard_map/all_gather | solution.py:84
  619.2 828.2 %all-gather.26.cloned.1.call-start = ((), (), s32[]{:S(2)}) async-start(), calls=%async_computation.12 | async-start | bytes 7077888 | tf_op jit(solution)/shard_map/all_gather | solution.py:91
  619.9 938.6 %all-gather.24.cloned.1.call-start = ((), (), s32[]{:S(2)}) async-start(), calls=%async_computation.11 | async-start | bytes 7077888 | tf_op jit(solution)/shard_map/all_gather | solution.py:90
  620.7 1027.2 %all-gather.28.cloned.1.call-start = ((), (), s32[]{:S(2)}) async-start(), calls=%async_computation.13 | async-start | bytes 7077888 | tf_op jit(solution)/shard_map/all_gather | solution.py:92
  621.4 1357.8 %all-gather.38.cloned.1.call-start = ((), (), s32[]{:S(2)}) async-start(), calls=%async_computation.23 | async-start | bytes 4227072 | tf_op jit(solution)/shard_map/all_gather | solution.py:85
  1352.6 939.0 %all-gather.40.cloned.1.call-start = ((), (), s32[]{:S(2)}) async-start(), calls=%async_computation.24 | async-start | bytes 4227072 | tf_op jit(solution)/shard_map/all_gather | solution.py:86
  1446.8 1154.0 %all-gather.42.cloned.1.call-start = ((), (), s32[]{:S(2)}) async-start(), calls=%async_computation.25 | async-start | bytes 4227072 | tf_op jit(solution)/shard_map/all_gather | solution.py:87
  1676.8 948.5 %all-to-all-start.3 = ((bf16[16,4,24,1536]{3,2,1,0:T(8,128)(2,1)}), bf16[16,4,24,1536]{3,2,1,0:T(8,128)(2,1)}, u32[]{:S(2)}, u32[]{:S(2)}) async-start(bf16[16,4,24,1536]{3,2,1,0:T(8,128)(2,1)} %copy.83), calls=%async_computation.3 | async-start | bytes 9437184 | tf_op jit(solution)/shard_map/all_to_all | solution.py:225
  1681.4 1665.0 %reduce-scatter.20.cloned.1.call-start = ((), (), s32[]{:S(2)}) async-start(), calls=%async_computation.14 | async-start | bytes 2228224 | tf_op jit(solution)/shard_map/reduce_scatter | solution.py:305
  2697.3 665.6 %reduce-scatter.22.cloned.1.call-start = ((), (), s32[]{:S(2)}) async-start(), calls=%async_computation.15 | async-start | bytes 2228224 | tf_op jit(solution)/shard_map/reduce_scatter | solution.py:311
  2701.1 2090.5 %reduce-scatter.24.cloned.1.call-start = ((), (), s32[]{:S(2)}) async-start(), calls=%async_computation.16 | async-start | bytes 7077888 | tf_op jit(solution)/shard_map/reduce_scatter | solution.py:229
  2709.6 2084.5 %reduce-scatter.26.cloned.1.call-start = ((), (), s32[]{:S(2)}) async-start(), calls=%async_computation.17 | async-start | bytes 7077888 | tf_op jit(solution)/shard_map/reduce_scatter | solution.py:232
  2719.8 2076.8 %reduce-scatter.28.cloned.1.call-start = ((), (), s32[]{:S(2)}) async-start(), calls=%async_computation.18 | async-start | bytes 7077888 | tf_op jit(solution)/shard_map/reduce_scatter | solution.py:235
  3225.0 1117.2 %all-to-all-start.1 = ((bf16[16,4,24,1536]{3,2,1,0:T(8,128)(2,1)}), bf16[16,4,24,1536]{3,2,1,0:T(8,128)(2,1)}, u32[]{:S(2)}, u32[]{:S(2)}) async-start(bf16[16,4,24,1536]{3,2,1,0:T(8,128)(2,1)} %copy.79), calls=%async_computation.1 | async-start | bytes 9437184 | tf_op jit(solution)/shard_map/all_to_all | solution.py:175
  3366.2 574.2 %collective-permute-start.196 = (f32[1024,16]{0,1:T(8,128)}, f32[1024,16]{0,1:T(8,128)}, u32[]{:S(2)}, u32[]{:S(2)}) collective-permute-start(f32[1024,16]{0,1:T(8,128)} %fusion.8), channel_id=1, source_target_pairs={{0,5},{1,6},{2,7},{3,8},{4,9},{5,10},{6,11},{7,12},{8,13},{9,14},{... | collective-permute-start | bytes 196616
  3369.2 572.5 %collective-permute-start.195 = (f32[1024,16]{0,1:T(8,128)}, f32[1024,16]{0,1:T(8,128)}, u32[]{:S(2)}, u32[]{:S(2)}) collective-permute-start(f32[1024,16]{0,1:T(8,128)} %fusion.8), channel_id=1, source_target_pairs={{0,4},{1,5},{2,6},{3,7},{4,8},{5,9},{6,10},{7,11},{8,12},{9,13},{1... | collective-permute-start | bytes 196616
  3372.5 570.5 %collective-permute-start.194 = (f32[1024,16]{0,1:T(8,128)}, f32[1024,16]{0,1:T(8,128)}, u32[]{:S(2)}, u32[]{:S(2)}) collective-permute-start(f32[1024,16]{0,1:T(8,128)} %fusion.8), channel_id=1, source_target_pairs={{0,3},{1,4},{2,5},{3,6},{4,7},{5,8},{6,9},{7,10},{8,11},{9,12},{10... | collective-permute-start | bytes 196616
  3374.7 569.6 %collective-permute-start.193 = (f32[1024,16]{0,1:T(8,128)}, f32[1024,16]{0,1:T(8,128)}, u32[]{:S(2)}, u32[]{:S(2)}) collective-permute-start(f32[1024,16]{0,1:T(8,128)} %fusion.8), channel_id=1, source_target_pairs={{0,2},{1,3},{2,4},{3,5},{4,6},{5,7},{6,8},{7,9},{8,10},{9,11},{10,... | collective-permute-start | bytes 196616
  3382.1 563.6 %collective-permute-start.192 = (f32[1024,16]{0,1:T(8,128)}, f32[1024,16]{0,1:T(8,128)}, u32[]{:S(2)}, u32[]{:S(2)}) collective-permute-start(f32[1024,16]{0,1:T(8,128)} %fusion.8), channel_id=1, source_target_pairs={{0,1},{1,2},{2,3},{3,4},{4,5},{5,6},{6,7},{7,8},{8,9},{9,10},{10,1... | collective-permute-start | bytes 196616
  (475 other events, 23647.2 us)
Sparse Core Ops, SparseCore 0:
  9.7 301.4 all-gather.29
  312.9 301.3 all-gather.33
  616.6 35.3 all-gather.19
  654.1 34.0 all-gather.21
  689.8 310.5 all-gather.31
  1001.9 311.1 all-gather.35
  1315.4 125.1 all-gather.25
  1442.9 115.6 all-gather.23
  1560.8 86.9 all-gather.27
  1649.4 329.7 all-gather.37
  1980.9 310.6 all-gather.39
  2293.1 307.6 all-gather.41
  2697.4 67.0 reduce-scatter.19
  2766.8 63.8 reduce-scatter.21
  2834.3 110.3 reduce-scatter.23
  2948.5 110.9 reduce-scatter.25
  3063.2 109.5 reduce-scatter.27
where the time goes:
time: 4830 us; the launch traced here: 4810 us
  waiting for transfers between devices  2390 us (49%)
  blocking collectives  1160 us (24%)
  starting transfers between devices  648 us (13%)
  local copies, waits for them, and re-layouts  396 us (8%)
  matrix products  146 us (3%)
    unnamed x4, blocking collectives  1160 us
    unnamed x224, starting transfers between devices  623 us
    all_gather x1, waiting for transfers between devices, local(): lax.all_gather(w_query, ('ctx', 'fsdp'), axis=0, tiled=True)  309 us
    all_gather x1, waiting for transfers between devices, local(): lax.all_gather(shared_up, ('ctx', 'fsdp'), axis=0, tiled=True)  306 us
    all_gather x1, waiting for transfers between devices, local(): lax.all_gather(shared_down, ('ctx', 'fsdp'), axis=1, tiled=True)  305 us
    unnamed x499, local copies, waits for them, and re-layouts  301 us
    all_gather x1, waiting for transfers between devices, local(): lax.all_gather(w_out, ('ctx', 'fsdp'), axis=1, tiled=True)  301 us
    all_gather x1, waiting for transfers between devices, local(): lax.all_gather(value_weight_matrix, ('ctx', 'fsdp'), axis=0, tiled=True)  299 us
  transfers between devices with their start and end apart: 245, of which 13 were waited for; matrix products, arithmetic and copies ran while one was open for 32% of the time, Pallas kernels for 0%

commit v1 on v0

v1 whole, which is shorter than its diff:
```python
import functools

import jax
import jax.numpy as jnp
from jax import lax
from jax.experimental import pallas as pl
from jax.experimental.pallas import tpu as pltpu
from jax.sharding import PartitionSpec as P

BF = jnp.bfloat16
F32 = jnp.float32
EPS = 1e-05
MESH = pl.DeviceIdType.MESH
ANY = pl.BlockSpec(memory_space=pl.ANY)
VM = pl.BlockSpec(memory_space=pltpu.VMEM)
SDS = jax.ShapeDtypeStruct
SCALE = 128 ** (-0.5)
VMEM_LIMIT = 56 * 2**20


def nn(a, b):
    return lax.dot_general(a, b, (((1,), (0,)), ((), ())), preferred_element_type=F32)


def nt(a, b):
    return lax.dot_general(a, b, (((1,), (1,)), ((), ())), preferred_element_type=F32)


def tn(a, b):
    return lax.dot_general(a, b, (((0,), (0,)), ((), ())), preferred_element_type=F32)


def silu_parts(pre_act):
    sig = 1.0 / (1.0 + jnp.exp(-pre_act))
    return pre_act * sig, sig * (1.0 + pre_act * (1.0 - sig))


def coords():
    c = lax.axis_index("ctx")
    f = lax.axis_index("fsdp")
    return c // 4, (c // 2) % 2, c % 2, f // 4, f % 4


def dev(y, xl, co, xh, z):
    return (y * 4 + xl * 2 + co, xh * 4 + z)


def barrier(peers):
    sem = pltpu.get_barrier_semaphore()
    for peer in peers:
        pl.semaphore_signal(sem, inc=1, device_id=peer, device_id_type=MESH)
    pl.semaphore_wait(sem, len(peers))


class Copies:
    def __init__(self, send, recv):
        self.send, self.recv, self.n, self.started = send, recv, 0, []

    def start(self, src, dst, peer):
        copy = pltpu.make_async_remote_copy(
            src, dst, self.send.at[self.n], self.recv.at[self.n], device_id=peer, device_id_type=MESH
        )
        copy.start()
        self.n += 1
        self.started.append(copy)
        return copy

    def finish(self, received=()):
        for copy in self.started:
            copy.wait_send()
            if not any(copy is r for r in received):
                copy.wait_recv()


def remote(kernel, outs, ins, copies, local, cid, scratch=()):
    return pl.pallas_call(
        kernel,
        out_shape=outs,
        in_specs=[ANY] * len(ins),
        out_specs=jax.tree.map(lambda _: ANY, outs),
        scratch_shapes=[
            pltpu.SemaphoreType.DMA((copies,)),
            pltpu.SemaphoreType.DMA((copies,)),
            pltpu.SemaphoreType.DMA((local,)),
        ]
        + list(scratch),
        compiler_params=pltpu.CompilerParams(
            collective_id=cid, has_side_effects=True, vmem_limit_bytes=VMEM_LIMIT
        ),
    )(*ins)


Y_STEPS = (1, 2, 3)
F_STEPS = tuple((dx, dz) for dx in (0, 1) for dz in range(4) if (dx, dz) != (0, 0))
C_STEPS = tuple((dy, dx) for dy in range(4) for dx in (0, 1) if (dy, dx) != (0, 0))


def gather_start_kernel(
    a_in, b_in, tok, cot, rg, wf, bfull, tokf, cotf, rgf, a2, b1, send, recv, loc
):
    y, xl, co, xh, z = coords()
    c, f = y * 4 + xl * 2 + co, xh * 4 + z
    sib = dev(y, xl, 1 - co, xh, z)
    xpeer = dev(y, 1 - xl, co, xh, z)
    fpeers = [dev(y, xl, co, (xh + dx) % 2, (z + dz) % 4) for dx, dz in F_STEPS]
    cpeers = [
        ((y + dy) % 4, (xl + dx) % 2, (co + dc) % 2)
        for dy in range(4)
        for dx in (0, 1)
        for dc in (0, 1)
        if (dy, dx, dc) != (0, 0, 0)
    ]
    barrier([dev(*p, xh, z) for p in cpeers] + fpeers)
    cp = Copies(send, recv)
    got = []
    lc = [
        pltpu.make_async_copy(a_in.at[y], a2.at[y, xl], loc.at[0]),
        pltpu.make_async_copy(b_in.at[c], b1.at[c], loc.at[1]),
        pltpu.make_async_copy(tok, tokf.at[y], loc.at[2]),
        pltpu.make_async_copy(cot, cotf.at[c], loc.at[3]),
        pltpu.make_async_copy(rg, rgf.at[c], loc.at[4]),
    ]
    for copy in lc:
        copy.start()
    first = [
        cp.start(a_in.at[(y + d) % 4], a2.at[y, xl], dev((y + d) % 4, xl, co, xh, z))
        for d in Y_STEPS
    ]
    bs = [cp.start(b_in.at[p[0] * 4 + p[1] * 2 + p[2]], b1.at[c], dev(*p, xh, z)) for p in cpeers]
    for d in Y_STEPS:
        cp.start(tok, tokf.at[y], dev((y + d) % 4, xl, co, xh, z))
    for p in cpeers:
        cp.start(rg, rgf.at[c], dev(*p, xh, z))
    lc[0].wait()
    for copy in first:
        copy.wait_recv()
        got.append(copy)
    xc = cp.start(a2.at[:, xl], a2.at[:, xl], xpeer)
    cots = [
        cp.start(cot, cotf.at[c], dev((y + dy) % 4, (xl + dx) % 2, co, xh, z)) for dy, dx in C_STEPS
    ]
    cp.start(cot, cotf.at[c], sib)
    xc.wait_recv()
    got.append(xc)
    lw = pltpu.make_async_copy(a2, wf.at[:, :, co, f], loc.at[5])
    lw.start()
    ws = [cp.start(a2, wf.at[:, :, co, f], p) for p in fpeers]
    lc[1].wait()
    for copy in bs:
        copy.wait_recv()
        got.append(copy)
    lb = pltpu.make_async_copy(b1, bfull.at[:, f], loc.at[6])
    lb.start()
    for p in fpeers:
        cp.start(b1, bfull.at[:, f], p)
    lw.wait()
    cp.start(wf.at[:, :, co, f], wf.at[:, :, co, f], sib)
    for (dx, dz), copy in zip(F_STEPS, ws):
        copy.wait_recv()
        got.append(copy)
        part = wf.at[:, :, co, ((xh + dx) % 2) * 4 + (z + 4 - dz) % 4]
        cp.start(part, part, sib)
    for (dy, dx), copy in zip(C_STEPS, cots):
        copy.wait_recv()
        got.append(copy)
        part = cotf.at[((y + 4 - dy) % 4) * 4 + ((xl + dx) % 2) * 2 + co]
        cp.start(part, part, sib)
    for copy in (lc[2], lc[3], lc[4], lb):
        copy.wait()
    cp.finish(got)


def gather_start(a_in, b_in, tok, cot, rg):
    n = a_in.shape[2]
    outs = (
        SDS((4, 2, 2, 8, 16, n), BF),
        SDS((16, 8, 16, b_in.shape[2]), BF),
        SDS((4,) + tok.shape, BF),
        SDS((16,) + cot.shape, BF),
        SDS((16,) + rg.shape, F32),
        SDS((4, 2, 16, n), BF),
        SDS((16, 16, b_in.shape[2]), BF),
    )
    return remote(gather_start_kernel, outs, (a_in, b_in, tok, cot, rg), 84, 8, 1)[:5]


def kv_gather_kernel(kv, out, send, recv, loc):
    y, xl, co, xh, z = coords()
    sib = dev(y, xl, 1 - co, xh, z)
    xpeer = dev(y, 1 - xl, co, xh, z)
    barrier([sib, xpeer])
    cp = Copies(send, recv)
    lc = pltpu.make_async_copy(kv, out.at[:, xl * 2 + co], loc.at[0])
    lc.start()
    a = cp.start(kv, out.at[:, xl * 2 + co], xpeer)
    cp.start(kv, out.at[:, xl * 2 + co], sib)
    a.wait_recv()
    part = out.at[:, (1 - xl) * 2 + co]
    cp.start(part, part, sib)
    lc.wait()
    cp.finish([a])


def kv_gather(kv):
    return remote(kv_gather_kernel, SDS((4, 4) + kv.shape[1:], BF), (kv,), 3, 1, 2)


def kv_scatter_kernel(dkv, out, send, recv, loc):
    y, xl, co, xh, z = coords()
    i = xl * 2 + co
    peers = [(1 - xl, co), (1 - xl, 1 - co), (xl, 1 - co)]
    barrier([dev(y, *p, xh, z) for p in peers])
    cp = Copies(send, recv)
    for p in peers:
        cp.start(dkv.at[:, p[0] * 2 + p[1]], out.at[i], dev(y, *p, xh, z))
    lc = pltpu.make_async_copy(dkv.at[:, i], out.at[i], loc.at[0])
    lc.start()
    lc.wait()
    cp.finish()


def kv_scatter(dkv):
    return remote(kv_scatter_kernel, SDS(dkv.shape, BF), (dkv,), 3, 1, 3)


def exchange_y_kernel(x, out, send, recv, loc):
    y, xl, co, xh, z = coords()
    peers = [dev((y + d) % 4, xl, co, xh, z) for d in Y_STEPS]
    barrier(peers)
    cp = Copies(send, recv)
    for d, p in zip(Y_STEPS, peers):
        cp.start(x.at[(y + d) % 4], out.at[y], p)
    lc = pltpu.make_async_copy(x.at[y], out.at[y], loc.at[0])
    lc.start()
    lc.wait()
    cp.finish()


def exchange_y(x, cid):
    return remote(exchange_y_kernel, SDS(x.shape, x.dtype), (x,), 3, 1, cid)


def gather_y_kernel(x, out, send, recv, loc):
    y, xl, co, xh, z = coords()
    peers = [dev((y + d) % 4, xl, co, xh, z) for d in Y_STEPS]
    barrier(peers)
    cp = Copies(send, recv)
    for p in peers:
        cp.start(x, out.at[y], p)
    lc = pltpu.make_async_copy(x, out.at[y], loc.at[0])
    lc.start()
    lc.wait()
    cp.finish()


def gather_y(x, cid):
    return remote(gather_y_kernel, SDS((4,) + x.shape, x.dtype), (x,), 3, 1, cid)


def gather_ctx_kernel(x, out, send, recv, loc):
    y, xl, co, xh, z = coords()
    c = y * 4 + xl * 2 + co
    sib = dev(y, xl, 1 - co, xh, z)
    peers = [dev((y + dy) % 4, (xl + dx) % 2, co, xh, z) for dy, dx in C_STEPS]
    barrier(peers + [sib])
    cp = Copies(send, recv)
    first = [cp.start(x, out.at[c], p) for p in peers]
    cp.start(x, out.at[c], sib)
    lc = pltpu.make_async_copy(x, out.at[c], loc.at[0])
    lc.start()
    for (dy, dx), copy in zip(C_STEPS, first):
        copy.wait_recv()
        part = out.at[((y + 4 - dy) % 4) * 4 + ((xl + dx) % 2) * 2 + co]
        cp.start(part, part, sib)
    lc.wait()
    cp.finish(first)


def gather_ctx(x, cid):
    return remote(gather_ctx_kernel, SDS((16,) + x.shape, x.dtype), (x,), 15, 1, cid)


def reduce_ctx_kernel(x, out, send, recv, loc, mine, theirs, got, total):
    y, xl, co, xh, z = coords()
    chip = y * 2 + xl
    sib = dev(y, xl, 1 - co, xh, z)
    peers = [((y + dy) % 4, (xl + dx) % 2) for dy, dx in C_STEPS]
    barrier([dev(*p, co, xh, z) for p in peers] + [sib])
    cp = Copies(send, recv)
    order = [p[0] * 2 + p[1] for p in peers] + [chip]
    loads, sibs = [], []
    for k, other in enumerate(order):
        copy = pltpu.make_async_copy(x.at[other, co], mine.at[k], loc.at[k])
        copy.start()
        loads.append(copy)
        sibs.append(cp.start(x.at[other, 1 - co], theirs.at[k], sib))
    outgoing = []
    for k, p in enumerate(peers):
        loads[k].wait()
        sibs[k].wait_recv()
        mine[k] = (mine[k].astype(F32) + theirs[k].astype(F32)).astype(BF)
        outgoing.append(cp.start(mine.at[k], got.at[k], dev(*p, co, xh, z)))
    loads[7].wait()
    sibs[7].wait_recv()
    total[...] = mine[7].astype(F32) + theirs[7].astype(F32)
    for k, copy in enumerate(outgoing):
        copy.wait_recv()
        total[...] += got[k].astype(F32)
    store = pltpu.make_async_copy(total, out, loc.at[8])
    store.start()
    store.wait()
    cp.finish(sibs + outgoing)


def reduce_ctx(x, cid):
    rows, width = x.shape[1:]
    x = x.reshape(8, 2, rows, width)
    scratch = [pltpu.VMEM((8, rows, width), BF)] * 2 + [
        pltpu.VMEM((7, rows, width), BF),
        pltpu.VMEM((rows, width), F32),
    ]
    return remote(reduce_ctx_kernel, SDS((rows, width), F32), (x,), 15, 9, cid, scratch)


def grads_end_kernel(
    da, db, gh, aout, bout, ghout, send, recv, loc, mine, theirs, fgot, s2, xgot, s3, bgot, bmine, sb
):
    y, xl, co, xh, z = coords()
    c, f = y * 4 + xl * 2 + co, xh * 4 + z
    sib = dev(y, xl, 1 - co, xh, z)
    xpeer = dev(y, 1 - xl, co, xh, z)
    fsteps = [((xh + dx) % 2, (z + dz) % 4) for dx, dz in F_STEPS]
    cpeers = [
        ((y + dy) % 4, (xl + dx) % 2, (co + dc) % 2)
        for dy in range(4)
        for dx in (0, 1)
        for dc in (0, 1)
        if (dy, dx, dc) != (0, 0, 0)
    ]
    barrier([dev(*p, xh, z) for p in cpeers] + [dev(y, xl, co, *p) for p in fsteps])
    cp = Copies(send, recv)
    got = []
    load = pltpu.make_async_copy(da.at[:, :, co], mine, loc.at[0])
    load.start()
    bload = pltpu.make_async_copy(db.at[:, f], bmine, loc.at[1])
    bload.start()
    glocal = pltpu.make_async_copy(gh.at[y], ghout.at[y], loc.at[2])
    glocal.start()
    sc = cp.start(da.at[:, :, 1 - co], theirs, sib)
    for d in Y_STEPS:
        cp.start(gh.at[(y + d) % 4], ghout.at[y], dev((y + d) % 4, xl, co, xh, z))
    bs = [
        cp.start(db.at[:, p[0] * 4 + p[1]], bgot.at[k], dev(y, xl, co, *p))
        for k, p in enumerate(fsteps)
    ]
    load.wait()
    sc.wait_recv()
    got.append(sc)
    for a in range(4):
        for b in range(2):
            mine[a, b] = (mine[a, b].astype(F32) + theirs[a, b].astype(F32)).astype(BF)
    fs = [
        cp.start(mine.at[:, :, p[0] * 4 + p[1]], fgot.at[k], dev(y, xl, co, *p))
        for k, p in enumerate(fsteps)
    ]
    bload.wait()
    for copy in bs:
        copy.wait_recv()
        got.append(copy)
    for a in range(16):
        tot = bmine[a].astype(F32)
        for k in range(7):
            tot = tot + bgot[k, a].astype(F32)
        sb[a] = tot.astype(BF)
    for p in cpeers:
        cp.start(sb.at[p[0] * 4 + p[1] * 2 + p[2]], bout.at[c], dev(*p, xh, z))
    bl = pltpu.make_async_copy(sb.at[c], bout.at[c], loc.at[3])
    bl.start()
    for copy in fs:
        copy.wait_recv()
        got.append(copy)
    for a in range(4):
        for b in range(2):
            tot = mine[a, b, f].astype(F32)
            for k in range(7):
                tot = tot + fgot[k, a, b].astype(F32)
            s2[b, a] = tot.astype(BF)
    xc = cp.start(s2.at[1 - xl], xgot, xpeer)
    xc.wait_recv()
    got.append(xc)
    for a in range(4):
        s3[a] = (s2[xl, a].astype(F32) + xgot[a].astype(F32)).astype(BF)
    for d in Y_STEPS:
        cp.start(s3.at[(y + d) % 4], aout.at[y], dev((y + d) % 4, xl, co, xh, z))
    al = pltpu.make_async_copy(s3.at[y], aout.at[y], loc.at[4])
    al.start()
    for copy in (glocal, bl, al):
        copy.wait()
    cp.finish(got)


def grads_end(da, db, gh):
    n, m = da.shape[-1], db.shape[-1]
    outs = (SDS((4, 16, n), BF), SDS((16, 16, m), BF), SDS(gh.shape, BF))
    scratch = [
        pltpu.VMEM((4, 2, 8, 16, n), BF),
        pltpu.VMEM((4, 2, 8, 16, n), BF),
        pltpu.VMEM((7, 4, 2, 16, n), BF),
        pltpu.VMEM((2, 4, 16, n), BF),
        pltpu.VMEM((4, 16, n), BF),
        pltpu.VMEM((4, 16, n), BF),
        pltpu.VMEM((7, 16, 16, m), BF),
        pltpu.VMEM((16, 16, m), BF),
        pltpu.VMEM((16, 16, m), BF),
    ]
    return remote(grads_end_kernel, outs, (da, db, gh), 40, 5, 4, scratch)


def head_rows(ref, j):
    return jnp.concatenate([ref[j * 128 : (j + 1) * 128, h * 128 : (h + 1) * 128] for h in range(3)], 0)


def causal(scores, j):
    n = scores.shape[1]
    i = lax.axis_index("ctx") % 4
    row = lax.broadcasted_iota(jnp.int32, (384, n), 0) % 128
    col = lax.broadcasted_iota(jnp.int32, (384, n), 1)
    return col <= j * 512 + i * 128 + row


def attention_kernel(q_ref, kv_ref, o_ref, att_ref, lse_ref):
    for j in range(4):
        n = (j + 1) * 512
        s = nt(head_rows(q_ref, j), kv_ref[:n, :128]) * SCALE
        s = jnp.where(causal(s, j), s, -1e30)
        m = jnp.max(s, -1, keepdims=True)
        p = jnp.exp(s - m)
        total = jnp.sum(p, -1, keepdims=True)
        o = nn(p.astype(BF), kv_ref[:n, 128:]) / total
        for h in range(3):
            part = o[h * 128 : (h + 1) * 128]
            o_ref[j * 128 : (j + 1) * 128, h * 128 : (h + 1) * 128] = part
            att_ref[j * 128 : (j + 1) * 128, h * 128 : (h + 1) * 128] = part.astype(BF)
        lse_ref[j] = jnp.broadcast_to(m + jnp.log(total), (384, 128))


def attention(q, kv):
    return pl.pallas_call(
        attention_kernel,
        out_shape=(SDS((512, 384), F32), SDS((512, 384), BF), SDS((4, 384, 128), F32)),
        in_specs=[VM, VM],
        out_specs=(VM, VM, VM),
        compiler_params=pltpu.CompilerParams(vmem_limit_bytes=VMEM_LIMIT),
        cost_estimate=pl.CostEstimate(flops=2 * 10**9, bytes_accessed=4 * 10**6, transcendentals=2 * 10**6),
    )(q, kv)


def attention_back_kernel(q_ref, kv_ref, o_ref, lse_ref, go_ref, dq_ref, dkv_ref, dk, dv):
    dk[...] = jnp.zeros_like(dk)
    dv[...] = jnp.zeros_like(dv)
    for j in range(4):
        n = (j + 1) * 512
        q = head_rows(q_ref, j)
        go = head_rows(go_ref, j)
        delta = jnp.sum(head_rows(o_ref, j) * go.astype(F32), -1, keepdims=True)
        lse = lse_ref[j][:, :1]
        s = nt(q, kv_ref[:n, :128]) * SCALE
        p = jnp.where(causal(s, j), jnp.exp(s - lse), 0.0)
        dp = nt(go, kv_ref[:n, 128:])
        gs = (p * (dp - delta)).astype(BF)
        dv[:n] += tn(p.astype(BF), go)
        dk[:n] += tn(gs, q)
        dq = nn(gs, kv_ref[:n, :128]) * SCALE
        for h in range(3):
            dq_ref[j * 128 : (j + 1) * 128, h * 128 : (h + 1) * 128] = dq[
                h * 128 : (h + 1) * 128
            ].astype(BF)
    dkv_ref[:, :128] = (dk[...] * SCALE).astype(BF)
    dkv_ref[:, 128:] = dv[...].astype(BF)


def attention_back(q, kv, o, lse, go):
    return pl.pallas_call(
        attention_back_kernel,
        out_shape=(SDS((512, 384), BF), SDS((2048, 256), BF)),
        in_specs=[VM] * 5,
        out_specs=(VM, VM),
        scratch_shapes=[pltpu.VMEM((2048, 128), F32), pltpu.VMEM((2048, 128), F32)],
        compiler_params=pltpu.CompilerParams(vmem_limit_bytes=VMEM_LIMIT),
        cost_estimate=pl.CostEstimate(flops=5 * 10**9, bytes_accessed=8 * 10**6, transcendentals=2 * 10**6),
    )(q, kv, o, lse, go)


def dispatch_kernel(h2_ref, cot_ref, rg_ref, x_ref, gy_ref, pick_ref, gated_ref):
    first = lax.axis_index("ctx") * 4
    masks, gates = [], []
    for e in range(4):
        ms, gs = [], []
        for s in range(2):
            hit = jnp.where(rg_ref[s, 0:6] == (first + e).astype(F32), 1.0, 0.0)
            ms.append(jnp.sum(hit, 0, keepdims=True))
            gs.append(jnp.sum(hit * rg_ref[s, 8:14], 0, keepdims=True))
        masks.append(jnp.concatenate(ms, 1))
        gates.append(jnp.concatenate(gs, 1))
    mask = jnp.concatenate(masks + [jnp.zeros((4, 256), F32)], 0)
    before = lax.broadcasted_iota(jnp.int32, (256, 256), 0)
    after = lax.broadcasted_iota(jnp.int32, (256, 256), 1)
    tri = jnp.where((before <= after) & (before // 128 == after // 128), 1.0, 0.0).astype(BF)
    place = nn(mask.astype(BF), tri) - 1.0
    lane = lax.broadcasted_iota(jnp.int32, (1, 256), 1)
    slot = lax.broadcasted_iota(jnp.int32, (48, 256), 0).astype(F32)
    picks, gated = [], []
    for e in range(4):
        at = place[e : e + 1] + jnp.where(lane >= 128, 24.0, 0.0)
        at = jnp.where(masks[e] > 0.0, at, -1.0)
        hit = jnp.where(slot == at, 1.0, 0.0)
        picks.append(hit)
        gated.append(hit * gates[e])
    pick = jnp.concatenate(picks, 0).astype(BF)
    gate = jnp.concatenate(gated, 0).astype(BF)
    x_ref[...] = nn(pick, h2_ref[...].reshape(256, 1536)).astype(BF).reshape(4, 1, 48, 1536)
    gy_ref[...] = nn(gate, cot_ref[...].reshape(256, 1536)).astype(BF).reshape(4, 1, 48, 1536)
    pick_ref[0] = pick
    gated_ref[0] = gate


def dispatch(h2, cot, rg):
    rows = pl.BlockSpec((2, 128, 1536), lambda p: (p, 0, 0))
    slots = pl.BlockSpec((4, 1, 48, 1536), lambda p: (0, p, 0, 0))
    picks = pl.BlockSpec((1, 192, 256), lambda p: (p, 0, 0))
    return pl.pallas_call(
        dispatch_kernel,
        grid=(8,),
        out_shape=(SDS((4, 8, 48, 1536), BF),) * 2 + (SDS((8, 192, 256), BF),) * 2,
        in_specs=[rows, rows, pl.BlockSpec((2, 16, 128), lambda p: (p, 0, 0))],
        out_specs=(slots, slots, picks, picks),
        compiler_params=pltpu.CompilerParams(vmem_limit_bytes=VMEM_LIMIT),
        cost_estimate=pl.CostEstimate(flops=3 * 10**9, bytes_accessed=24 * 10**6, transcendentals=0),
    )(h2, cot, rg)


def piece_places():
    f = lax.axis_index("fsdp")
    xh, z = f // 4, f % 4
    steps = ((0, 0),) + F_STEPS
    source = [((xh + dx) % 2) * 4 + (z + 4 - dz) % 4 for dx, dz in steps]
    target = [((xh + dx) % 2) * 4 + (z + dz) % 4 for dx, dz in steps]
    return source, target


def expert_kernel(*refs):
    x_ref, gy_ref = refs[:2]
    pieces = refs[2:10]
    y_ref, gr_ref = refs[10:12]
    grads = refs[12:20]
    w, dw, u_s, ga_s, gb_s = refs[20:]
    source, target = piece_places()
    for k in range(8):
        w[:, pl.ds(pl.multiple_of(source[k] * 192, 192), 192), :] = pieces[k][:, 0]

    for t in range(2):
        cols = slice(t * 256, (t + 1) * 256)
        a = nn(x_ref[0], w[0, :, cols])
        b = nn(x_ref[0], w[1, :, cols])
        gu = nn(gy_ref[0], w[2, :, cols])
        act, slope = silu_parts(a)
        u_s[:, cols] = (act * b).astype(BF)
        ga_s[:, cols] = (gu * b * slope).astype(BF)
        gb_s[:, cols] = (gu * act).astype(BF)

    def tile(t, carry):
        at = pl.ds(pl.multiple_of(t * 256, 256), 256)
        y_ref[0, :, at] = nt(u_s[...], w[2, at, :]).astype(BF)
        gr_ref[0, :, at] = (nt(ga_s[...], w[0, at, :]) + nt(gb_s[...], w[1, at, :])).astype(BF)
        dw[0, at, :] = tn(x_ref[0, :, at], ga_s[...]).astype(BF)
        dw[1, at, :] = tn(x_ref[0, :, at], gb_s[...]).astype(BF)
        dw[2, at, :] = tn(gy_ref[0, :, at], u_s[...]).astype(BF)
        return carry

    lax.fori_loop(0, 6, tile, 0)
    for k in range(8):
        grads[k][:, 0] = dw[:, pl.ds(pl.multiple_of(target[k] * 192, 192), 192), :]


def expert(x, gy, pieces):
    rows = pl.BlockSpec((1, 384, 1536), lambda e: (e, 0, 0))
    piece = pl.BlockSpec((3, 1, 192, 512), lambda e: (0, e, 0, 0))
    out = pl.pallas_call(
        expert_kernel,
        grid=(4,),
        out_shape=(SDS((4, 384, 1536), BF),) * 2 + (SDS((3, 4, 192, 512), BF),) * 8,
        in_specs=[rows, rows] + [piece] * 8,
        out_specs=(rows, rows) + (piece,) * 8,
        scratch_shapes=[
            pltpu.VMEM((3, 1536, 512), BF),
            pltpu.VMEM((3, 1536, 512), BF),
            pltpu.VMEM((384, 512), BF),
            pltpu.VMEM((384, 512), BF),
            pltpu.VMEM((384, 512), BF),
        ],
        compiler_params=pltpu.CompilerParams(vmem_limit_bytes=VMEM_LIMIT),
        cost_estimate=pl.CostEstimate(flops=22 * 10**9, bytes_accessed=60 * 10**6, transcendentals=10**6),
    )(x, gy, *pieces)
    return out[0], out[1], out[2:]


def combine_kernel(pick_ref, gated_ref, y_ref, gr_ref, h2_ref, cot_ref, sw_ref, out_ref, gh_ref, ds_ref):
    @pl.when(pl.program_id(0) == 0)
    def _():
        ds_ref[...] = jnp.zeros_like(ds_ref)

    h2 = h2_ref[...].reshape(256, 1536)
    cot = cot_ref[...].reshape(256, 1536)
    act, slope = silu_parts(nn(h2, sw_ref[:, 0:128]))
    up = nn(h2, sw_ref[:, 128:256])
    gz = nn(cot, sw_ref[:, 256:384])
    hid = (act * up).astype(BF)
    gc = (gz * up * slope).astype(BF)
    gd = (gz * act).astype(BF)
    out = tn(gated_ref[0], y_ref[...].reshape(192, 1536)) + nt(hid, sw_ref[:, 256:384])
    out_ref[...] = out.astype(BF).reshape(2, 128, 1536)
    gh = tn(pick_ref[0], gr_ref[...].reshape(192, 1536)) + nt(gc, sw_ref[:, 0:128])
    gh = gh + nt(gd, sw_ref[:, 128:256])
    gh_ref[...] = gh.astype(BF).reshape(2, 128, 1536)
    ds_ref[:, 0:128] += tn(h2, gc)
    ds_ref[:, 128:256] += tn(h2, gd)
    ds_ref[:, 256:384] += tn(cot, hid)


def combine(pick, gated, y, gr, h2, cot, sw):
    rows = pl.BlockSpec((2, 128, 1536), lambda p: (p, 0, 0))
    slots = pl.BlockSpec((4, 1, 48, 1536), lambda p: (0, p, 0, 0))
    picks = pl.BlockSpec((1, 192, 256), lambda p: (p, 0, 0))
    whole = pl.BlockSpec((1536, 384), lambda p: (0, 0))
    return pl.pallas_call(
        combine_kernel,
        grid=(8,),
        out_shape=(SDS((16, 128, 1536), BF),) * 2 + (SDS((1536, 384), F32),),
        in_specs=[picks, picks, slots, slots, rows, rows, whole],
        out_specs=(rows, rows, whole),
        compiler_params=pltpu.CompilerParams(vmem_limit_bytes=VMEM_LIMIT),
        cost_estimate=pl.CostEstimate(flops=8 * 10**9, bytes_accessed=36 * 10**6, transcendentals=10**6),
    )(pick, gated, y, gr, h2, cot, sw)


def norm_forward(values, gain_vec):
    inverse = lax.rsqrt(jnp.mean(values * values, -1, keepdims=True) + EPS)
    scaled = values * inverse
    return scaled * gain_vec, scaled, inverse


def norm_row_grad(grad_in, scaled, inverse, gain_vec):
    inner = grad_in * gain_vec
    return inverse * (inner - scaled * jnp.mean(inner * scaled, -1, keepdims=True))


def pack_rows():
    row = jnp.arange(96)[:, None]
    col = jnp.arange(128)[None, :]
    return ((row // 12) * 16 + row % 12 == col).astype(BF)


def local(
    tokens,
    cotangent,
    routes,
    gates,
    attn_gain,
    ffn_gain,
    w_query,
    w_key,
    w_value,
    w_out,
    shared_gate,
    shared_up,
    shared_down,
    expert_gate,
    expert_up,
    expert_down,
):
    tok = tokens.reshape(128, 1536)
    cot = cotangent.reshape(128, 1536)
    rg = jnp.concatenate(
        [
            jnp.pad(routes.reshape(128, 6).T.astype(F32), ((0, 2), (0, 0)), constant_values=-1.0),
            jnp.pad(gates.reshape(128, 6).T, ((0, 2), (0, 0))),
        ],
        0,
    )
    gains = jnp.pad(jnp.stack([attn_gain, ffn_gain], 1), ((0, 0), (0, 126)))
    a_in = jnp.concatenate(
        [
            w_query.reshape(12, 4, 384),
            w_key.reshape(12, 4, 128),
            w_value.reshape(12, 4, 128),
            w_out.T.reshape(12, 4, 384),
            jnp.broadcast_to(gains[:, None], (12, 4, 128)),
        ],
        2,
    )
    a_in = jnp.pad(jnp.transpose(a_in, (1, 0, 2)), ((0, 0), (0, 4), (0, 0)))
    b_in = jnp.concatenate(
        [
            shared_gate.reshape(12, 16, 64),
            shared_up.reshape(12, 16, 64),
            shared_down.T.reshape(12, 16, 64),
            jnp.zeros((12, 16, 64), BF),
        ],
        2,
    )
    b_in = jnp.pad(jnp.transpose(b_in, (1, 0, 2)), ((0, 0), (0, 4), (0, 0)))
    w_raw, b_raw, tok_f, cot_f, rg_f = gather_start(a_in, b_in, tok, cot, rg)

    own = jnp.stack([expert_gate, expert_up, jnp.transpose(expert_down, (0, 2, 1))])
    own, w_raw = lax.optimization_barrier((own, w_raw))
    pieces = [own] + [
        lax.ppermute(
            own, "fsdp", [(f, ((f // 4 + dx) % 2) * 4 + (f % 4 + dz) % 4) for f in range(8)]
        )
        for dx, dz in F_STEPS
    ]

    pack = pack_rows()
    w = jnp.einsum("ap,cpn->can", pack, w_raw.reshape(16, 128, 1152), preferred_element_type=F32)
    w = w.astype(BF).reshape(1536, 1152)
    sw = jnp.einsum("ap,cpn->can", pack, b_raw.reshape(16, 128, 256), preferred_element_type=F32)
    sw = sw.astype(BF).reshape(1536, 256)
    sw = jnp.pad(sw[:, :192].reshape(1536, 3, 64), ((0, 0), (0, 0), (0, 64))).reshape(1536, 384)
    w_qkv, w_o = w[:, :640], w[:, 640:1024]
    gain_one, gain_two = w[:, 1024].astype(F32), w[:, 1025].astype(F32)

    h1, xh1, _ = norm_forward(tok_f.reshape(512, 1536).astype(F32), gain_one)
    h1 = h1.astype(BF)
    qkv = nn(h1, w_qkv).astype(BF)
    q = qkv[:, :384]
    kv = kv_gather(qkv[:, 384:].reshape(4, 128, 256)).reshape(2048, 256)
    o, attended, lse = attention(q, kv)
    partial = nt(attended, w_o).astype(BF).reshape(4, 128, 1536)
    inputs = tok.astype(F32)
    resid = inputs + jnp.sum(exchange_y(partial, 5).astype(F32), 0)
    h2, xh2, inv2 = norm_forward(resid, gain_two)
    h2_f = gather_ctx(h2.astype(BF), 6)

    x, gy, pick, gated = dispatch(h2_f, cot_f, rg_f)
    y, gr, egrads = expert(x.reshape(4, 384, 1536), gy.reshape(4, 384, 1536), pieces)
    out_p, gh2_p, ds = combine(
        pick, gated, y.reshape(4, 8, 48, 1536), gr.reshape(4, 8, 48, 1536), h2_f, cot_f, sw
    )
    sums = egrads[0].astype(F32)
    for (dx, dz), piece in zip(F_STEPS, egrads[1:]):
        sums = sums + lax.ppermute(
            piece, "fsdp", [(f, ((f // 4 + dx) % 2) * 4 + (f % 4 + dz) % 4) for f in range(8)]
        ).astype(F32)

    gh2 = reduce_ctx(gh2_p, 7)
    gain_two_grad = jnp.sum(gh2 * xh2, 0)
    gresid = cot.astype(F32) + norm_row_grad(gh2, xh2, inv2, gain_two)
    gattn = gather_y(gresid.astype(BF), 8).reshape(512, 1536)
    layer_out = (resid + reduce_ctx(out_p, 9)).astype(BF)

    go = nn(gattn, w_o).astype(BF)
    dw_o = tn(gattn, attended)
    dq, dkv = attention_back(q, kv, o, lse, go)
    dkv = jnp.sum(kv_scatter(dkv.reshape(4, 4, 128, 256)).astype(F32), 0).astype(BF)
    gqkv = jnp.concatenate([dq, dkv.reshape(512, 256)], 1)
    gh1_p = nt(gqkv, w_qkv)
    dw_qkv = tn(h1, gqkv)
    gain_one_grad = jnp.sum(gh1_p * xh1, 0)
    gain_grads = jnp.pad(jnp.stack([gain_one_grad, gain_two_grad], 1), ((0, 0), (0, 126)))
    da = jnp.concatenate([dw_qkv, dw_o, gain_grads], 1).astype(BF).reshape(16, 96, 1152)
    da = jnp.einsum("ap,can->cpn", pack, da, preferred_element_type=F32).astype(BF)
    db = jnp.pad(ds.reshape(1536, 3, 128)[:, :, :64].reshape(1536, 192), ((0, 0), (0, 64)))
    db = db.astype(BF).reshape(16, 96, 256)
    db = jnp.einsum("ap,can->cpn", pack, db, preferred_element_type=F32).astype(BF)
    a_out, b_out, gh1 = grads_end(
        da.reshape(4, 2, 2, 8, 16, 1152),
        db.reshape(16, 8, 16, 256),
        gh1_p.astype(BF).reshape(4, 128, 1536),
    )
    gh1 = jnp.sum(gh1.astype(F32), 0)
    _, xh1_own, inv1 = norm_forward(inputs, gain_one)
    input_grad = gresid + norm_row_grad(gh1, xh1_own, inv1, gain_one)

    a_out = jnp.transpose(a_out[:, :12].astype(F32), (1, 0, 2))
    b_out = jnp.transpose(b_out[:, :12].astype(F32), (1, 0, 2))
    gain_out = jnp.sum(a_out[:, :, 1024:1026], 1)
    return (
        layer_out.reshape(1, 128, 1536),
        input_grad.reshape(1, 128, 1536),
        gain_out[:, 0],
        gain_out[:, 1],
        a_out[:, :, 0:384].reshape(12, 1536),
        a_out[:, :, 384:512].reshape(12, 512),
        a_out[:, :, 512:640].reshape(12, 512),
        a_out[:, :, 640:1024].reshape(12, 1536).T,
        b_out[:, :, 0:64].reshape(12, 1024),
        b_out[:, :, 64:128].reshape(12, 1024),
        b_out[:, :, 128:192].reshape(12, 1024).T,
        sums[0],
        sums[1],
        jnp.transpose(sums[2], (0, 2, 1)),
    )


def solution(mesh):
    both = ("ctx", "fsdp")
    rows = P("fsdp", "ctx", None)
    weights = (P(both),) * 2 + (P(both, None),) * 3 + (P(None, both),)
    weights = weights + (P(both, None),) * 2 + (P(None, both),)
    weights = weights + (P("ctx", "fsdp", None),) * 2 + (P("ctx", None, "fsdp"),)
    return jax.shard_map(
        local, mesh=mesh, in_specs=(rows,) * 4 + weights, out_specs=(rows,) * 2 + weights, check_vma=False
    )
```

time: 4830 us -> 1060 us (0.22)
  waiting for transfers between devices: 2390 us -> 267 us
  blocking collectives: 1160 us -> 0 us
  Pallas kernels: 0 us -> 649 us
  starting transfers between devices: 648 us -> 38.5 us
  local copies, waits for them, and re-layouts: 396 us -> 37.8 us
  matrix products: 146 us -> 23.3 us
    all_gather x12 -> x0, waiting for transfers between devices: 2290 us -> none  [the longest x1 309 us: local(): lax.all_gather(w_query, ('ctx', 'fsdp'), axis=0, tiled=True)]
    unnamed x4 -> x0, blocking collectives: 1160 us -> none
    pallas_call x0 -> x14, Pallas kernels: none -> 649 us  [the longest x9 558 us: remote(): pl.pallas_call(kernel, out_shape=outs, in_specs=[ANY] * len(ins), out_spe...]
    unnamed x224 -> x0, starting transfers between devices: 623 us -> none
    unnamed x499 -> x79, local copies, waits for them, and re-layouts: 301 us -> 7.65 us
    ppermute x0 -> x14, waiting for transfers between devices: none -> 267 us  [the longest x7 183 us: local(): lax.ppermute(own, 'fsdp', [(f, (f // 4 + dx) % 2 * 4 + (f % 4 + dz) % 4)...]
    dot_general x52 -> x10, matrix products: 146 us -> 23.3 us  [the longest x2 7.41 us: nt(): lax.dot_general(a, b, (((1,), (1,)), ((), ())), preferred_element_type=F32)]
    all_to_all x4 -> x0, waiting for transfers between devices: 64.2 us -> none  [the longest x1 64.2 us: local(): lax.all_to_all(outgoing.reshape(ctx_size, exp_dev, capacity, model_width)...]
  transfers between devices with their start and end apart: 245 -> 14, of which waited for: 13 -> 4; matrix products, arithmetic and copies ran while one was open for 32% -> 5% of each run, Pallas kernels for 0% -> 39%
where the time goes in v1:
time: 1060 us; the launch traced here: 1040 us
  Pallas kernels  649 us (61%)
  waiting for transfers between devices  267 us (25%)
  starting transfers between devices  38.5 us (4%)
  local copies, waits for them, and re-layouts  37.8 us (4%)
  other arithmetic  27.4 us (3%)
  matrix products  23.3 us (2%)
    pallas_call x9, Pallas kernels, remote(): pl.pallas_call(kernel, out_shape=outs, in_specs=[ANY] * len(ins), out_spe...  558 us
    ppermute x7, waiting for transfers between devices, local(): lax.ppermute(own, 'fsdp', [(f, (f // 4 + dx) % 2 * 4 + (f % 4 + dz) % 4)...  183 us
    ppermute x7, waiting for transfers between devices, local(): lax.ppermute(piece, 'fsdp', [(f, (f // 4 + dx) % 2 * 4 + (f % 4 + dz) % 4...  84.3 us
    pallas_call x1, Pallas kernels, expert(): pl.pallas_call(expert_kernel, grid=(4,), out_shape=(SDS((4, 384, 1536), B...  38.8 us
    pallas_call x1, Pallas kernels, combine(): pl.pallas_call(combine_kernel, grid=(8,), out_shape=(SDS((16, 128, 1536),...  23.3 us
    ppermute x7, starting transfers between devices, local(): lax.ppermute(piece, 'fsdp', [(f, (f // 4 + dx) % 2 * 4 + (f % 4 + dz) % 4...  21.8 us
  transfers between devices with their start and end apart: 14, of which 4 were waited for; matrix products, arithmetic and copies ran while one was open for 5% of the time, Pallas kernels for 39%

profile of v1, /device:TPU:0, one launch (start us, length us, event | category | flops | bytes accessed | tf_op | source)
XLA Modules:
  0.0 1044.8 jit_solution(2170345114968141986)
XLA Ops:
  13.8 90.2 %shard_map.263 = (bf16[4,2,2,8,16,1152]{5,4,3,2,1,0:T(8,128)(2,1)}, bf16[16,8,16,256]{3,2,1,0:T(8,128)(2,1)}, bf16[4,128,1536]{2,1,0:T(8,128)(2,1)}, bf16[16,128...) custom-call(bf16[4,16,1152]{2,1,0:T(8,128)(2,1)} %pad.35.a_in, ...), custom_call_target="tpu_custom_call" | custom-call | tf_op jit(solution)/shard_map/pallas_call | solution.py:76
  120.2 38.3 %collective-permute-done.refs_3_ = bf16[3,4,192,512]{3,2,1,0:T(8,128)(2,1)} collective-permute-done((bf16[3,4,192,512]{3,2,1,0:T(8,128)(2,1)}, bf16[3,4,192,512]{3,2,1,0:T(8,128)(2,1)}, u32[]{:S(2)}, u32[]{:S(2)}) %collective-permute-start) | collective-permute-done | bytes 2359328 | tf_op jit(solution)/shard_map/ppermute | solution.py:717
  158.6 7.1 collective-permute-start.5
  165.7 144.2 %collective-permute-done.1.refs_4_ = bf16[3,4,192,512]{3,2,1,0:T(8,128)(2,1)} collective-permute-done((bf16[3,4,192,512]{3,2,1,0:T(8,128)(2,1)}, bf16[3,4,192,512]{3,2,1,0:T(8,128)(2,1)}, u32[]{:S(2)}, u32[]{:S(2)}) %collective-permute-start.1) | collective-permute-done | bytes 2359328 | tf_op jit(solution)/shard_map/ppermute | solution.py:717
  313.1 53.3 %shard_map.264 = bf16[4,4,128,256]{3,2,1,0:T(8,128)(2,1)} custom-call(bf16[4,128,256]{2,1,0:T(8,128)(2,1)} %bitcast.158), custom_call_target="tpu_custom_call" | custom-call | tf_op jit(solution)/shard_map/pallas_call | solution.py:76
  366.4 7.0 shard_map.265
  376.6 30.4 %shard_map.266 = bf16[4,128,1536]{2,1,0:T(8,128)(2,1)} custom-call(bf16[4,128,1536]{2,1,0:T(8,128)(2,1)} %bitcast.155), custom_call_target="tpu_custom_call" | custom-call | tf_op jit(solution)/shard_map/pallas_call | solution.py:76
  410.7 41.4 %shard_map.267.h2_ref = bf16[16,128,1536]{2,1,0:T(8,128)(2,1)} custom-call(bf16[128,1536]{1,0:T(8,128)(2,1)} %multiply_convert_fusion.1.x), custom_call_target="tpu_custom_call" | custom-call | tf_op jit(solution)/shard_map/pallas_call | solution.py:76
  461.2 12.7 %shard_map.268 = (bf16[4,8,48,1536]{3,2,1,0:T(8,128)(2,1)}, bf16[4,8,48,1536]{3,2,1,0:T(8,128)(2,1)}, bf16[8,192,256]{2,1,0:T(8,128)(2,1)}, bf16[8,192,256]{2,1,0:T(8,128)(2,1)}) custom-call(bf16[16,128,1536]{2,1,0:T(8,128)(2,1)} %shard_map.267.h2_ref, bf16[16,128,1536]{2,1,0:T(8,128)(2,1)} %get-tuple-element.50.cot_ref, f32[16,16,128]{2,1,0:T(8,128)} %get-tuple-element.51.rg_ref), custom_call_target="tpu_custom_call" | custom-call | flops 3000000000 | bytes 24000000 | tf_op jit(solution)/shard_map/pallas_call | solution.py:531
  474.0 38.8 %shard_map.269 = (bf16[4,384,1536]{2,1,0:T(8,128)(2,1)}, bf16[4,384,1536]{2,1,0:T(8,128)(2,1)}, bf16[3,4,192,512]{3,2,1,0:T(8,128)(2,1)}, bf16[3,4,192,512]{3,2,...) custom-call(bf16[4,384,1536]{2,1,0:T(8,128)(2,1)} %bitcast.180, ...), custom_call_target="tpu_custom_call" | custom-call | flops 22000001024 | bytes 60000000 | tf_op jit(solution)/shard_map/pallas_call | solution.py:588
  512.8 23.3 %shard_map.270 = (bf16[16,128,1536]{2,1,0:T(8,128)(2,1)}, bf16[16,128,1536]{2,1,0:T(8,128)(2,1)}, f32[1536,384]{1,0:T(8,128)}) custom-call(bf16[8,192,256]{2,1,0:T(8,128)(2,1)} %get-tuple-element.52.pick_ref, bf16[8,192,256]{2,1,0:T(8,128)(2,1)} %get-tuple-element.53.gated_ref, bf16[4,8,48,1536]{3,2,1,0:T(8,128)(2,1)} %bitcast.184, ...), custom_call_target="tpu_custom_call" | custom-call | flops 8000000000 | bytes 36000000 | tf_op jit(solution)/shard_map/pallas_call | solution.py:635
  536.1 43.2 %shard_map.272 = f32[128,1536]{1,0:T(8,128)} custom-call(bf16[8,2,128,1536]{3,2,1,0:T(8,128)(2,1)} %bitcast.132), custom_call_target="tpu_custom_call" | custom-call | tf_op jit(solution)/shard_map/pallas_call | solution.py:76
  583.0 22.1 %shard_map.273 = bf16[4,128,1536]{2,1,0:T(8,128)(2,1)} custom-call(bf16[128,1536]{1,0:T(8,128)(2,1)} %fusion.40.x), custom_call_target="tpu_custom_call" | custom-call | tf_op jit(solution)/shard_map/pallas_call | solution.py:76
  605.1 3.5 convolution_convert_fusion.7.go_ref
  611.4 9.4 shard_map.274
  620.8 14.2 %shard_map.275 = bf16[4,4,128,256]{3,2,1,0:T(8,128)(2,1)} custom-call(bf16[4,4,128,256]{3,2,1,0:T(8,128)(2,1)} %bitcast.160), custom_call_target="tpu_custom_call" | custom-call | tf_op jit(solution)/shard_map/pallas_call | solution.py:76
  639.0 4.3 fusion.42
  648.5 125.9 %shard_map.271 = f32[128,1536]{1,0:T(8,128)} custom-call(bf16[8,2,128,1536]{3,2,1,0:T(8,128)(2,1)} %bitcast.131), custom_call_target="tpu_custom_call" | custom-call | tf_op jit(solution)/shard_map/pallas_call | solution.py:76
  774.5 7.0 collective-permute-start.11
  793.5 137.4 %shard_map.276 = (bf16[4,16,1152]{2,1,0:T(8,128)(2,1)}, bf16[16,16,256]{2,1,0:T(8,128)(2,1)}, bf16[4,128,1536]{2,1,0:T(8,128)(2,1)}) custom-call(bf16[4,2,2,8,16,1152]{5,4,3,2,1,0:T(8,128)(2,1)} %bitcast.143, bf16[16,8,16,256]{3,2,1,0:T(8,128)(2,1)} %bitcast.145, bf16[4,128,1536]{2,1,0:T(8,128)(2,1)} %bitcast.152), custom_call_target="tpu_custom_call" | custom-call | tf_op jit(solution)/shard_map/pallas_call | solution.py:76
  932.8 6.4 collective-permute-start.7
  951.0 37.0 %collective-permute-done.8 = bf16[3,4,192,512]{3,2,1,0:T(8,128)(2,1)} collective-permute-done((bf16[3,4,192,512]{3,2,1,0:T(8,128)(2,1)}, bf16[3,4,192,512]{3,2,1,0:T(8,128)(2,1)}, u32[]{:S(2)}, u32[]{:S(2)}) %collective-permute-start.8) | collective-permute-done | bytes 2359328 | tf_op jit(solution)/shard_map/ppermute | solution.py:751
  988.0 47.2 %collective-permute-done.7 = bf16[3,4,192,512]{3,2,1,0:T(8,128)(2,1)} collective-permute-done((bf16[3,4,192,512]{3,2,1,0:T(8,128)(2,1)}, bf16[3,4,192,512]{3,2,1,0:T(8,128)(2,1)}, u32[]{:S(2)}, u32[]{:S(2)}) %collective-permute-start.7) | collective-permute-done | bytes 2359328 | tf_op jit(solution)/shard_map/ppermute | solution.py:751
  1035.3 7.0 convert_add_fusion
  (180 shorter events, 91.7 us)
Async XLA Ops:
  104.0 54.6 %collective-permute-start = (bf16[3,4,192,512]{3,2,1,0:T(8,128)(2,1)}, bf16[3,4,192,512]{3,2,1,0:T(8,128)(2,1)}, u32[]{:S(2)}, u32[]{:S(2)}) collective-permute-start(bf16[3,4,192,512]{3,2,1,0:T(8,128)(2,1)} %pad_maximum_fusion.refs_2_), channel_id=1, source_target_pairs={{0,1},{1,2},{2,3},{3,0},{4,5},{5,6},{6,7},{7,4},{8,9},{9,10},{10,1... | collective-permute-start | bytes 7077896 | tf_op jit(solution)/shard_map/ppermute | solution.py:717
  106.4 203.6 %collective-permute-start.1 = (bf16[3,4,192,512]{3,2,1,0:T(8,128)(2,1)}, bf16[3,4,192,512]{3,2,1,0:T(8,128)(2,1)}, u32[]{:S(2)}, u32[]{:S(2)}) collective-permute-start(bf16[3,4,192,512]{3,2,1,0:T(8,128)(2,1)} %pad_maximum_fusion.refs_2_), channel_id=1, source_target_pairs={{0,2},{1,3},{2,0},{3,1},{4,6},{5,7},{6,4},{7,5},{8,10},{9,11},{10,... | collective-permute-start | bytes 7077896 | tf_op jit(solution)/shard_map/ppermute | solution.py:717
  108.3 365.7 %collective-permute-start.2 = (bf16[3,4,192,512]{3,2,1,0:T(8,128)(2,1)}, bf16[3,4,192,512]{3,2,1,0:T(8,128)(2,1)}, u32[]{:S(2)}, u32[]{:S(2)}) collective-permute-start(bf16[3,4,192,512]{3,2,1,0:T(8,128)(2,1)} %pad_maximum_fusion.refs_2_), channel_id=1, source_target_pairs={{0,3},{1,0},{2,1},{3,2},{4,7},{5,4},{6,5},{7,6},{8,11},{9,8},{10,9... | collective-permute-start | bytes 7077896 | tf_op jit(solution)/shard_map/ppermute | solution.py:717
  110.8 363.1 %collective-permute-start.3 = (bf16[3,4,192,512]{3,2,1,0:T(8,128)(2,1)}, bf16[3,4,192,512]{3,2,1,0:T(8,128)(2,1)}, u32[]{:S(2)}, u32[]{:S(2)}) collective-permute-start(bf16[3,4,192,512]{3,2,1,0:T(8,128)(2,1)} %pad_maximum_fusion.refs_2_), channel_id=1, source_target_pairs={{0,4},{1,5},{2,6},{3,7},{4,0},{5,1},{6,2},{7,3},{8,12},{9,13},{10,... | collective-permute-start | bytes 7077896 | tf_op jit(solution)/shard_map/ppermute | solution.py:717
  111.5 362.4 %collective-permute-start.4 = (bf16[3,4,192,512]{3,2,1,0:T(8,128)(2,1)}, bf16[3,4,192,512]{3,2,1,0:T(8,128)(2,1)}, u32[]{:S(2)}, u32[]{:S(2)}) collective-permute-start(bf16[3,4,192,512]{3,2,1,0:T(8,128)(2,1)} %pad_maximum_fusion.refs_2_), channel_id=1, source_target_pairs={{0,5},{1,6},{2,7},{3,4},{4,1},{5,2},{6,3},{7,0},{8,13},{9,14},{10,... | collective-permute-start | bytes 7077896 | tf_op jit(solution)/shard_map/ppermute | solution.py:717
  119.4 190.8 %copy-start.5 = (bf16[16,1152,96]{1,2,0:T(8,128)(2,1)S(1)}, bf16[16,1152,96]{1,2,0:T(8,128)(2,1)}, u32[]{:S(2)}) copy-start(bf16[16,1152,96]{1,2,0:T(8,128)(2,1)} %copy-done.4) | copy-start | bytes 10616836
  119.8 191.8 %copy-start.20 = (f32[512]{0:T(512)}, f32[512]{0:T(512)S(1)}, u32[]{:S(2)}) copy-start(f32[512]{0:T(512)S(1)} %rsqrt_bitcast_fusion) | copy-start | bytes 6148
  120.2 191.4 %copy-start.3 = (bf16[512,1536]{1,0:T(8,128)(2,1)}, bf16[512,1536]{1,0:T(8,128)(2,1)S(1)}, u32[]{:S(2)}) copy-start(bf16[512,1536]{1,0:T(8,128)(2,1)S(1)} %multiply_convert_fusion) | copy-start | bytes 4718596
  158.6 315.4 %collective-permute-start.5 = (bf16[3,4,192,512]{3,2,1,0:T(8,128)(2,1)}, bf16[3,4,192,512]{3,2,1,0:T(8,128)(2,1)}, u32[]{:S(2)}, u32[]{:S(2)}) collective-permute-start(bf16[3,4,192,512]{3,2,1,0:T(8,128)(2,1)} %pad_maximum_fusion.refs_2_), channel_id=1, source_target_pairs={{0,6},{1,7},{2,4},{3,5},{4,2},{5,3},{6,0},{7,1},{8,14},{9,15},{10,... | collective-permute-start | bytes 7077896 | tf_op jit(solution)/shard_map/ppermute | solution.py:717
  309.9 164.1 %collective-permute-start.6 = (bf16[3,4,192,512]{3,2,1,0:T(8,128)(2,1)}, bf16[3,4,192,512]{3,2,1,0:T(8,128)(2,1)}, u32[]{:S(2)}, u32[]{:S(2)}) collective-permute-start(bf16[3,4,192,512]{3,2,1,0:T(8,128)(2,1)} %pad_maximum_fusion.refs_2_), channel_id=1, source_target_pairs={{0,7},{1,4},{2,5},{3,6},{4,3},{5,0},{6,1},{7,2},{8,15},{9,12},{10,... | collective-permute-start | bytes 7077896 | tf_op jit(solution)/shard_map/ppermute | solution.py:717
  409.8 42.3 %copy-start.17 = (f32[128]{0:T(128)}, f32[128]{0:T(128)S(1)}, u32[]{:S(2)}) copy-start(f32[128]{0:T(128)S(1)} %get-tuple-element.102) | copy-start | bytes 1540
  536.1 43.3 %copy-start.18 = (f32[128]{0:T(128)S(1)}, f32[128]{0:T(128)}, u32[]{:S(2)}) copy-start(f32[128]{0:T(128)} %copy-done.17) | copy-start | bytes 1540
  536.1 44.7 %copy-start.6 = (bf16[1,128,1536]{2,1,0:T(8,128)(2,1)S(1)}, bf16[1,128,1536]{2,1,0:T(8,128)(2,1)}, u32[]{:S(2)}) copy-start(bf16[1,128,1536]{2,1,0:T(8,128)(2,1)} %param.17) | copy-start | bytes 1179652
  636.4 295.5 %collective-permute-start.13 = (bf16[3,4,192,512]{3,2,1,0:T(8,128)(2,1)}, bf16[3,4,192,512]{3,2,1,0:T(8,128)(2,1)}, u32[]{:S(2)}, u32[]{:S(2)}) collective-permute-start(bf16[3,4,192,512]{3,2,1,0:T(8,128)(2,1)} %get-tuple-element.77), channel_id=1, source_target_pairs={{0,7},{1,4},{2,5},{3,6},{4,3},{5,0},{6,1},{7,2},{8,15},{9,12},{10,... | collective-permute-start | bytes 7077896 | tf_op jit(solution)/shard_map/ppermute | solution.py:751
  637.5 295.3 %collective-permute-start.12 = (bf16[3,4,192,512]{3,2,1,0:T(8,128)(2,1)}, bf16[3,4,192,512]{3,2,1,0:T(8,128)(2,1)}, u32[]{:S(2)}, u32[]{:S(2)}) collective-permute-start(bf16[3,4,192,512]{3,2,1,0:T(8,128)(2,1)} %get-tuple-element.76), channel_id=1, source_target_pairs={{0,6},{1,7},{2,4},{3,5},{4,2},{5,3},{6,0},{7,1},{8,14},{9,15},{10,... | collective-permute-start | bytes 7077896 | tf_op jit(solution)/shard_map/ppermute | solution.py:751
  648.5 137.9 %copy-start.25 = (s32[96]{0:T(128)S(1)}, s32[96]{0:T(128)}, u32[]{:S(2)}) copy-start(s32[96]{0:T(128)} %copy-done.23) | copy-start | bytes 1156
  648.5 139.4 %copy-start.10 = (bf16[512,1536]{0,1:T(8,128)(2,1)S(1)}, bf16[512,1536]{0,1:T(8,128)(2,1)}, u32[]{:S(2)}) copy-start(bf16[512,1536]{0,1:T(8,128)(2,1)} %copy.96) | copy-start | bytes 4718596
  648.5 139.4 %copy-start.28 = (bf16[512,384]{1,0:T(8,128)(2,1)S(1)}, bf16[512,384]{1,0:T(8,128)(2,1)}, u32[]{:S(2)}) copy-start(bf16[512,384]{1,0:T(8,128)(2,1)} %get-tuple-element.49) | copy-start | bytes 1179652
  774.5 176.5 %collective-permute-start.11 = (bf16[3,4,192,512]{3,2,1,0:T(8,128)(2,1)}, bf16[3,4,192,512]{3,2,1,0:T(8,128)(2,1)}, u32[]{:S(2)}, u32[]{:S(2)}) collective-permute-start(bf16[3,4,192,512]{3,2,1,0:T(8,128)(2,1)} %get-tuple-element.75), channel_id=1, source_target_pairs={{0,5},{1,6},{2,7},{3,4},{4,1},{5,2},{6,3},{7,0},{8,13},{9,14},{10,... | collective-permute-start | bytes 7077896 | tf_op jit(solution)/shard_map/ppermute | solution.py:751
  781.5 169.5 %collective-permute-start.10 = (bf16[3,4,192,512]{3,2,1,0:T(8,128)(2,1)}, bf16[3,4,192,512]{3,2,1,0:T(8,128)(2,1)}, u32[]{:S(2)}, u32[]{:S(2)}) collective-permute-start(bf16[3,4,192,512]{3,2,1,0:T(8,128)(2,1)} %get-tuple-element.74), channel_id=1, source_target_pairs={{0,4},{1,5},{2,6},{3,7},{4,0},{5,1},{6,2},{7,3},{8,12},{9,13},{10,... | collective-permute-start | bytes 7077896 | tf_op jit(solution)/shard_map/ppermute | solution.py:751
  783.5 167.5 %collective-permute-start.9 = (bf16[3,4,192,512]{3,2,1,0:T(8,128)(2,1)}, bf16[3,4,192,512]{3,2,1,0:T(8,128)(2,1)}, u32[]{:S(2)}, u32[]{:S(2)}) collective-permute-start(bf16[3,4,192,512]{3,2,1,0:T(8,128)(2,1)} %get-tuple-element.73), channel_id=1, source_target_pairs={{0,3},{1,0},{2,1},{3,2},{4,7},{5,4},{6,5},{7,6},{8,11},{9,8},{10,9... | collective-permute-start | bytes 7077896 | tf_op jit(solution)/shard_map/ppermute | solution.py:751
  931.9 56.1 %collective-permute-start.8 = (bf16[3,4,192,512]{3,2,1,0:T(8,128)(2,1)}, bf16[3,4,192,512]{3,2,1,0:T(8,128)(2,1)}, u32[]{:S(2)}, u32[]{:S(2)}) collective-permute-start(bf16[3,4,192,512]{3,2,1,0:T(8,128)(2,1)} %get-tuple-element.72), channel_id=1, source_target_pairs={{0,2},{1,3},{2,0},{3,1},{4,6},{5,7},{6,4},{7,5},{8,10},{9,11},{10,... | collective-permute-start | bytes 7077896 | tf_op jit(solution)/shard_map/ppermute | solution.py:751
  932.8 102.5 %collective-permute-start.7 = (bf16[3,4,192,512]{3,2,1,0:T(8,128)(2,1)}, bf16[3,4,192,512]{3,2,1,0:T(8,128)(2,1)}, u32[]{:S(2)}, u32[]{:S(2)}) collective-permute-start(bf16[3,4,192,512]{3,2,1,0:T(8,128)(2,1)} %get-tuple-element.71), channel_id=1, source_target_pairs={{0,1},{1,2},{2,3},{3,0},{4,5},{5,6},{6,7},{7,4},{8,9},{9,10},{10,1... | collective-permute-start | bytes 7077896 | tf_op jit(solution)/shard_map/ppermute | solution.py:751
  949.6 85.7 %copy-start.8 = (bf16[3,4,192,512]{3,2,1,0:T(8,128)(2,1)S(1)}, bf16[3,4,192,512]{3,2,1,0:T(8,128)(2,1)}, u32[]{:S(2)}) copy-start(bf16[3,4,192,512]{3,2,1,0:T(8,128)(2,1)} %get-tuple-element.70) | copy-start | bytes 7077892
  (20 other events, 236.8 us)
